TPU v7x, 32 devices: a whole 2x2x4 slice. The times are simulated.
32 devices in a mesh: dp: 4 (over y, core), expert: 8 (over z, x).
Axes of the slice: x: 2, y: 2, z: 4, core: 2. Of those that a mesh axis runs over, the one named last changes fastest.
Arguments:
- tokens: bfloat16 [2, 8, 1024, 768], P(None, 'expert', 'dp'), may hold values from -6 to 6
- doc_lengths: int32 [2, 8, 4], P(None, 'expert'), may hold values from 1 to 1021, as said below
- routes: int32 [2, 8, 1024, 2], P(None, 'expert', 'dp'), may hold values from 0 to 7, as said below
- slots: int32 [2, 8, 1024, 2], P(None, 'expert', 'dp'), may hold values from -1 to 71, as said below
- w_qkv: bfloat16 [768, 2304], P(('dp', 'expert')), may hold values from -0.21875 to 0.21875
- w_out: bfloat16 [768, 768], P(('dp', 'expert')), may hold values from -1.75 to 1.75
- rel_bias: bfloat16 [1024, 12], replicated, may hold values from -4 to 4
- gain_attn: bfloat16 [768], P(('dp', 'expert')), may hold values from 0.5 to 1.5
- gain_ffn: bfloat16 [768], P(('dp', 'expert')), may hold values from 0.5 to 1.5
- w_router: bfloat16 [768, 8], P(('dp', 'expert')), may hold values from -0.15625 to 0.15625
- w_in: bfloat16 [8, 768, 3072], P('expert'), may hold values from -0.21875 to 0.21875
- w_back: bfloat16 [8, 3072, 768], P('expert'), may hold values from -0.109375 to 0.109375
- cotangent: bfloat16 [2, 8, 1024, 768], P(None, 'expert', 'dp'), may hold values from -6 to 6
Outputs:
- output: bfloat16 [2, 8, 1024, 768], P(None, 'expert', 'dp')
- token_grad: bfloat16 [2, 8, 1024, 768], P(None, 'expert', 'dp')
- grad_w_qkv: float32 [768, 2304], P(('dp', 'expert'))
- grad_w_out: float32 [768, 768], P(('dp', 'expert'))
- grad_rel_bias: float32 [1024, 12], replicated
- grad_gain_attn: float32 [768], P(('dp', 'expert'))
- grad_gain_ffn: float32 [768], P(('dp', 'expert'))
- grad_w_router: float32 [768, 8], P(('dp', 'expert'))
- grad_w_in: float32 [8, 768, 3072], P('expert', 'dp')
- grad_w_back: float32 [8, 3072, 768], P('expert', 'dp')
Inputs may be any that keep to these rules, and one draw needn't show every extreme that they name: `routes`: the 2 experts of a token differ. Among the pairs of one device and micro-batch that go to one expert, the kept ones hold the slots 0 to their count minus one without repeats, at most 72 of them; -1 marks a dropped pair. In every draw, for each micro-batch and dp index, some expert keeps 72 pairs from every device. `doc_lengths`: the 4 lengths of a sequence are positive and sum to 1024.
All inputs are finite; a program needn't handle non-finite values.
Results may differ from a plain program's by a relative error of at most 0.013.
Values may be sent and summed in bfloat16 or wider, within the bound.
No kernel may reach another device: no remote copies, remote signals or barrier semaphores. Data moves between devices by JAX's collectives and lax.ppermute only.
A program may use at most 256 MiB of HBM per device.

v0:
```python
import jax
import jax.numpy as jnp
from jax import lax
from jax.sharding import PartitionSpec as P

H = 12
HD = 64
TOP = 2
WINDOW = 1024


EPSILON = 1e-06
HIGHEST = lax.Precision.HIGHEST
MASKED = -1e30


def shifted(x, axis, by):
    peers = lax.axis_size(axis)
    pairs = [(i, i + by) for i in range(peers) if 0 <= i + by < peers]
    return lax.ppermute(x, axis, pairs)


def rms_scale(values, gain_vector):
    return (
        values
        * lax.rsqrt(jnp.mean(values * values, axis=-1, keepdims=True) + EPSILON)
        * gain_vector
    )


def doc_numbers(doc_ends, places):
    return jnp.sum((doc_ends[None, :] <= places[:, None]).astype(jnp.int32), axis=1)


def shear_band(band_row, height, breadth):
    extent = height + breadth - 1
    leading = band_row.shape[:-1]
    spread = jnp.broadcast_to(band_row[..., None, :], leading + (height, extent)).reshape(
        leading + (height * extent,)
    )
    spread = jnp.concatenate([spread, jnp.zeros(leading + (height,), band_row.dtype)], axis=-1)
    return spread.reshape(leading + (height, extent + 1))[..., :breadth]


def unshear(tiles):
    height = tiles.shape[-2]
    breadth = tiles.shape[-1]
    extent = height + breadth - 1
    leading = tiles.shape[:-2]
    padded = jnp.concatenate([tiles, jnp.zeros(leading + (height, height), tiles.dtype)], axis=-1)
    flattened = padded.reshape(leading + (height * (extent + 1),))[..., : height * extent]
    return jnp.sum(flattened.reshape(leading + (height, extent)), axis=-2)


def shards(
    tokens,
    doc_lengths,
    routes,
    slots,
    w_qkv,
    w_out,
    rel_bias,
    gain_attn,
    gain_ffn,
    w_router,
    w_in,
    w_back,
    cotangent,
):
    micro_count = tokens.shape[0]
    tok_rows = tokens.shape[2]
    model_width = tokens.shape[3]
    shard_index = lax.axis_index("dp")
    key_reach = min((WINDOW - 2) // tok_rows + 1, lax.axis_size("dp") - 1)
    expert_count = lax.axis_size("expert")
    capacity = (9 * tok_rows * TOP + 8 * expert_count - 1) // (8 * expert_count)
    key_count = (key_reach + 1) * tok_rows
    pair_count = tok_rows * TOP
    score_scale = HD ** (-0.5)
    ff_width = w_in.shape[2]
    bias_rows = rel_bias.astype(jnp.float32).T
    band_all = jnp.concatenate(
        [
            jnp.zeros((H, tok_rows - 1), jnp.float32),
            bias_rows,
            jnp.zeros((H, key_count - WINDOW), jnp.float32),
        ],
        axis=1,
    )
    query_pos = shard_index * tok_rows + jnp.arange(tok_rows, dtype=jnp.int32)
    key_pos = (shard_index - key_reach) * tok_rows + jnp.arange(key_count, dtype=jnp.int32)
    distance_grid = query_pos[:, None] - key_pos[None, :]
    window_ok = (distance_grid >= 0) & (distance_grid < WINDOW) & (key_pos[None, :] >= 0)
    expert_ids = jnp.arange(expert_count, dtype=jnp.int32)

    def collect_dense():
        return (
            lax.all_gather(w_qkv, ("dp", "expert"), axis=0, tiled=True),
            lax.all_gather(w_out, ("dp", "expert"), axis=0, tiled=True),
            lax.all_gather(w_router, ("dp", "expert"), axis=0, tiled=True),
            lax.all_gather(gain_attn, ("dp", "expert"), axis=0, tiled=True),
            lax.all_gather(gain_ffn, ("dp", "expert"), axis=0, tiled=True),
        )

    def group_scores(query_part, key_part, start_head, allowed):
        tiles = jnp.flip(
            shear_band(band_all[start_head : start_head + 4], tok_rows, key_count), axis=-1
        )
        raw_scores = (
            jnp.einsum("qhd,khd->hqk", query_part, key_part, preferred_element_type=jnp.float32)
            * score_scale
            + tiles
        )
        return jnp.where(allowed[None], raw_scores, MASKED)

    grad_qkv = jnp.zeros((model_width, 3 * model_width), jnp.float32)
    grad_out = jnp.zeros((model_width, model_width), jnp.float32)
    grad_router = jnp.zeros((model_width, expert_count), jnp.float32)
    grad_gain_attn = jnp.zeros((model_width,), jnp.float32)
    grad_gain_ffn = jnp.zeros((model_width,), jnp.float32)
    grad_in = jnp.zeros((model_width, ff_width), jnp.float32)
    grad_back = jnp.zeros((ff_width, model_width), jnp.float32)
    band_grad = jnp.zeros((H, tok_rows + key_count - 1), jnp.float32)
    outputs = []
    input_grads = []
    for micro in range(micro_count):
        dense_now = collect_dense()
        w_qkv_full, w_out_full, router_full, gain_attn_full, gain_ffn_full = dense_now
        doc_ends = jnp.cumsum(doc_lengths[micro, 0])
        allowed = window_ok & (
            doc_numbers(doc_ends, query_pos)[:, None] == doc_numbers(doc_ends, key_pos)[None, :]
        )
        inputs = tokens[micro, 0].astype(jnp.float32)
        normed_attn = rms_scale(inputs, gain_attn_full.astype(jnp.float32)).astype(jnp.bfloat16)
        qkv = jnp.dot(normed_attn, w_qkv_full, preferred_element_type=jnp.float32).astype(
            jnp.bfloat16
        )
        queries = qkv[:, :model_width]
        own_pairs = qkv[:, model_width:]
        earlier = [shifted(own_pairs, "dp", distance) for distance in range(key_reach, 0, -1)]
        key_value = jnp.concatenate(earlier + [own_pairs], axis=0)
        attended_parts = []
        lse_parts = []
        for start_head in range(0, H, 4):
            low_col = start_head * HD
            high_col = (start_head + 4) * HD
            query_part = queries[:, low_col:high_col].reshape(tok_rows, 4, HD)
            key_part = key_value[:, low_col:high_col].reshape(key_count, 4, HD)
            value_part = key_value[:, model_width + low_col : model_width + high_col].reshape(
                key_count, 4, HD
            )
            scores = group_scores(query_part, key_part, start_head, allowed)
            row_peak = jnp.max(scores, axis=-1, keepdims=True)
            exp_scores = jnp.exp(scores - row_peak)
            row_total = jnp.sum(exp_scores, axis=-1, keepdims=True)
            prob_low = (exp_scores / row_total).astype(jnp.bfloat16)
            lse_parts.append(row_peak + jnp.log(row_total))
            attended_parts.append(
                jnp.einsum(
                    "hqk,khd->qhd", prob_low, value_part, preferred_element_type=jnp.float32
                ).reshape(tok_rows, 4 * HD)
            )
        attended = jnp.concatenate(attended_parts, axis=1).astype(jnp.bfloat16)
        mixed = inputs + jnp.dot(attended, w_out_full, preferred_element_type=jnp.float32)
        normed_ffn = rms_scale(mixed, gain_ffn_full.astype(jnp.float32)).astype(jnp.bfloat16)
        logits = jnp.dot(normed_ffn, router_full, preferred_element_type=jnp.float32)
        route_now = routes[micro, 0]
        slot_now = slots[micro, 0]
        chooser = (route_now[:, :, None] == expert_ids[None, None, :]).astype(jnp.float32)
        chosen = jnp.einsum("te,tke->tk", logits, chooser, precision=HIGHEST)
        gate_values = jax.nn.softmax(chosen, axis=-1)
        places = jnp.where(
            slot_now >= 0, route_now * capacity + slot_now, expert_count * capacity
        ).reshape(-1)
        owners = (
            jnp.full((expert_count * capacity,), pair_count, jnp.int32)
            .at[places]
            .set(jnp.arange(pair_count, dtype=jnp.int32), mode="drop")
        )
        padded_rows = jnp.concatenate(
            [normed_ffn, jnp.zeros((1, model_width), jnp.bfloat16)], axis=0
        )
        outgoing = padded_rows[owners // TOP].reshape(expert_count, capacity, model_width)
        arrived_rows = lax.all_to_all(outgoing, "expert", split_axis=0, concat_axis=0, tiled=True)
        source_count = arrived_rows.shape[0]
        slot_count = arrived_rows.shape[1]
        flat_in = arrived_rows.reshape(source_count * slot_count, model_width)
        pre_act = jnp.dot(flat_in, w_in[0], preferred_element_type=jnp.float32)
        hidden = jax.nn.gelu(pre_act).astype(jnp.bfloat16)
        result = jnp.dot(hidden, w_back[0], preferred_element_type=jnp.float32).astype(jnp.bfloat16)
        result = result.reshape(source_count, slot_count, model_width)
        coming_back = lax.all_to_all(result, "expert", split_axis=0, concat_axis=0, tiled=True)
        pre_kept = pre_act.reshape(source_count, slot_count, ff_width)
        padded_back = jnp.concatenate(
            [
                coming_back.reshape(expert_count * capacity, model_width),
                jnp.zeros((1, model_width), jnp.bfloat16),
            ],
            axis=0,
        )
        pair_values = padded_back[places].reshape(tok_rows, TOP, model_width).astype(jnp.float32)
        moe_sum = jnp.sum(gate_values[..., None] * pair_values, axis=1)
        outputs.append((mixed + moe_sum).astype(jnp.bfloat16))
        w_qkv_back, w_out_back, router_back, gain_attn_back, gain_ffn_back = collect_dense()
        upstream = cotangent[micro, 0].astype(jnp.float32)
        gate_grad = jnp.einsum("td,tkd->tk", upstream, pair_values, precision=HIGHEST)
        chosen_grad = gate_values * (
            gate_grad - jnp.sum(gate_values * gate_grad, axis=-1, keepdims=True)
        )
        logit_grad = jnp.einsum("tk,tke->te", chosen_grad, chooser, precision=HIGHEST)
        grad_router = grad_router + jnp.dot(
            normed_ffn.astype(jnp.float32).T, logit_grad, precision=HIGHEST
        )
        router_term = jnp.dot(logit_grad, router_back.astype(jnp.float32).T, precision=HIGHEST)
        pair_grad = (
            (gate_values[..., None] * upstream[:, None, :])
            .astype(jnp.bfloat16)
            .reshape(pair_count, model_width)
        )
        padded_grad = jnp.concatenate(
            [pair_grad, jnp.zeros((1, model_width), jnp.bfloat16)], axis=0
        )
        outgoing_grad = padded_grad[owners].reshape(expert_count, capacity, model_width)
        arrived_grad = lax.all_to_all(
            outgoing_grad, "expert", split_axis=0, concat_axis=0, tiled=True
        )
        flat_grad = arrived_grad.reshape(-1, model_width)
        flat_in = arrived_rows.reshape(-1, model_width)
        flat_pre = pre_kept.reshape(-1, ff_width)
        hidden_float, gelu_back = jax.vjp(jax.nn.gelu, flat_pre)
        hidden = hidden_float.astype(jnp.bfloat16)
        grad_back = grad_back + jnp.dot(hidden.T, flat_grad, preferred_element_type=jnp.float32)
        hidden_grad = jnp.dot(flat_grad, w_back[0].T, preferred_element_type=jnp.float32)
        pre_grad = gelu_back(hidden_grad)[0].astype(jnp.bfloat16)
        grad_in = grad_in + jnp.dot(flat_in.T, pre_grad, preferred_element_type=jnp.float32)
        row_grad = jnp.dot(pre_grad, w_in[0].T, preferred_element_type=jnp.float32).astype(
            jnp.bfloat16
        )
        returned_grad = lax.all_to_all(
            row_grad.reshape(expert_count, capacity, model_width),
            "expert",
            split_axis=0,
            concat_axis=0,
            tiled=True,
        )
        padded_return = jnp.concatenate(
            [
                returned_grad.reshape(expert_count * capacity, model_width),
                jnp.zeros((1, model_width), jnp.bfloat16),
            ],
            axis=0,
        )
        token_pairs = padded_return[places].reshape(tok_rows, TOP, model_width).astype(jnp.float32)
        normed_ffn_grad = router_term + jnp.sum(token_pairs, axis=1)
        normed_again, ffn_norm_back = jax.vjp(rms_scale, mixed, gain_ffn_back.astype(jnp.float32))
        mixed_part, gain_ffn_part = ffn_norm_back(normed_ffn_grad)
        grad_gain_ffn = grad_gain_ffn + gain_ffn_part
        mixed_grad = upstream + mixed_part
        branch_grad = mixed_grad.astype(jnp.bfloat16)
        grad_out = grad_out + jnp.dot(attended.T, branch_grad, preferred_element_type=jnp.float32)
        attended_grad = jnp.dot(
            branch_grad, w_out_back.T, preferred_element_type=jnp.float32
        ).astype(jnp.bfloat16)
        query_grads = []
        key_grads = []
        value_grads = []
        band_parts = []
        for group_index, start_head in enumerate(range(0, H, 4)):
            low_col = start_head * HD
            high_col = (start_head + 4) * HD
            query_part = queries[:, low_col:high_col].reshape(tok_rows, 4, HD)
            key_part = key_value[:, low_col:high_col].reshape(key_count, 4, HD)
            value_part = key_value[:, model_width + low_col : model_width + high_col].reshape(
                key_count, 4, HD
            )
            grad_part = attended_grad[:, low_col:high_col].reshape(tok_rows, 4, HD)
            scores = group_scores(query_part, key_part, start_head, allowed)
            prob_float = jnp.exp(scores - lse_parts[group_index])
            prob_low = prob_float.astype(jnp.bfloat16)
            prob_grad = jnp.einsum(
                "qhd,khd->hqk", grad_part, value_part, preferred_element_type=jnp.float32
            )
            centre = jnp.sum(prob_float * prob_grad, axis=-1, keepdims=True)
            score_grad = (prob_float * (prob_grad - centre)).astype(jnp.bfloat16)
            band_parts.append(unshear(jnp.flip(score_grad.astype(jnp.float32), axis=-1)))
            value_grads.append(
                jnp.einsum(
                    "hqk,qhd->khd", prob_low, grad_part, preferred_element_type=jnp.float32
                ).reshape(key_count, 4 * HD)
            )
            key_grads.append(
                (
                    jnp.einsum(
                        "hqk,qhd->khd", score_grad, query_part, preferred_element_type=jnp.float32
                    )
                    * score_scale
                ).reshape(key_count, 4 * HD)
            )
            query_grads.append(
                (
                    jnp.einsum(
                        "hqk,khd->qhd", score_grad, key_part, preferred_element_type=jnp.float32
                    )
                    * score_scale
                ).reshape(tok_rows, 4 * HD)
            )
        band_grad = band_grad + jnp.concatenate(band_parts, axis=0)
        pair_grads = jnp.concatenate(key_grads + value_grads, axis=1)
        own_grad = pair_grads[key_reach * tok_rows :]
        for distance in range(1, key_reach + 1):
            block_rows = pair_grads[
                (key_reach - distance) * tok_rows : (key_reach - distance + 1) * tok_rows
            ]
            own_grad = own_grad + shifted(block_rows.astype(jnp.bfloat16), "dp", -distance).astype(
                block_rows.dtype
            )
        qkv_grad = jnp.concatenate(query_grads + [own_grad], axis=1).astype(jnp.bfloat16)
        grad_qkv = grad_qkv + jnp.dot(normed_attn.T, qkv_grad, preferred_element_type=jnp.float32)
        normed_attn_grad = jnp.dot(qkv_grad, w_qkv_back.T, preferred_element_type=jnp.float32)
        attn_again, attn_norm_back = jax.vjp(rms_scale, inputs, gain_attn_back.astype(jnp.float32))
        inputs_part, gain_attn_part = attn_norm_back(normed_attn_grad)
        grad_gain_attn = grad_gain_attn + gain_attn_part
        input_grads.append((mixed_grad + inputs_part).astype(jnp.bfloat16))
    dense_summed = (
        lax.psum_scatter(grad_qkv, ("dp", "expert"), scatter_dimension=0, tiled=True),
        lax.psum_scatter(grad_out, ("dp", "expert"), scatter_dimension=0, tiled=True),
        lax.psum_scatter(grad_router, ("dp", "expert"), scatter_dimension=0, tiled=True),
        lax.psum_scatter(grad_gain_attn, ("dp", "expert"), scatter_dimension=0, tiled=True),
        lax.psum_scatter(grad_gain_ffn, ("dp", "expert"), scatter_dimension=0, tiled=True),
    )
    expert_summed = (
        lax.psum_scatter(
            grad_in[None].astype(jnp.bfloat16), "dp", scatter_dimension=1, tiled=True
        ).astype(jnp.float32),
        lax.psum_scatter(
            grad_back[None].astype(jnp.bfloat16), "dp", scatter_dimension=1, tiled=True
        ).astype(jnp.float32),
    )
    bias_summed = lax.psum(band_grad[:, tok_rows - 1 : tok_rows - 1 + WINDOW].T, ("dp", "expert"))
    output = jnp.stack(outputs)[:, None]
    token_grad = jnp.stack(input_grads)[:, None]
    return (
        output,
        token_grad,
        dense_summed[0],
        dense_summed[1],
        bias_summed,
        dense_summed[3],
        dense_summed[4],
        dense_summed[2],
        expert_summed[0],
        expert_summed[1],
    )


def solution(mesh):
    return jax.shard_map(
        shards,
        mesh=mesh,
        in_specs=(
            P(None, "expert", "dp", None),
            P(None, "expert", None),
            P(None, "expert", "dp", None),
            P(None, "expert", "dp", None),
            P(("dp", "expert"), None),
            P(("dp", "expert"), None),
            P(),
            P(("dp", "expert")),
            P(("dp", "expert")),
            P(("dp", "expert"), None),
            P("expert", None, None),
            P("expert", None, None),
            P(None, "expert", "dp", None),
        ),
        out_specs=(
            P(None, "expert", "dp", None),
            P(None, "expert", "dp", None),
            P(("dp", "expert"), None),
            P(("dp", "expert"), None),
            P(),
            P(("dp", "expert")),
            P(("dp", "expert")),
            P(("dp", "expert"), None),
            P("expert", "dp", None),
            P("expert", "dp", None),
        ),
        check_vma=False,
    )
```

profile of v0, /device:TPU:0, one launch (start us, length us, event | category | flops | bytes accessed | tf_op | source)
XLA Modules:
  0.0 1592.3 jit_solution(8800505667136977535)
XLA Ops:
  10.4 42.4 %all-reduce.24 = (bf16[768]{0:T(1024)(128)(2,1)S(1)}, bf16[768]{0:T(1024)(128)(2,1)S(1)}) all-reduce(bf16[768]{0:T(1024)(128)(2,1)S(1)} %dynamic-update-slice, bf16[768]{0:T(1024)(128)(2,1)S(1)} %dynamic-update-slice.1), channel_id=1, replica_groups=mesh['dp'=4,'expert'=8] {'dp','expert'}, use_global_device_ids=true, to_apply=%add.18 | all-reduce | flops 1536 | bytes 6144
  76.1 34.6 %rev.37 = f32[4,256,1024]{2,1,0:T(8,128)} reverse(f32[4,256,1024]{2,1,0:T(8,128)} %slice.298), dimensions={2} | reverse | bytes 8388608 | tf_op jit(solution)/shard_map/jit(_flip)/rev | solution.py:106
  130.5 34.8 %rev.38 = f32[4,256,1024]{2,1,0:T(8,128)} reverse(f32[4,256,1024]{2,1,0:T(8,128)} %slice.302), dimensions={2} | reverse | bytes 8388608 | tf_op jit(solution)/shard_map/jit(_flip)/rev | solution.py:106
  185.1 34.4 %rev.39 = f32[4,256,1024]{2,1,0:T(8,128)} reverse(f32[4,256,1024]{2,1,0:T(8,128)} %slice.306), dimensions={2} | reverse | bytes 8388608 | tf_op jit(solution)/shard_map/jit(_flip)/rev | solution.py:106
  219.5 66.3 %all-gather = bf16[32,24,8]{1,2,0:T(8,128)(2,1)S(1)} all-gather(bf16[1,24,8]{1,2,0:T(8,128)(2,1)S(1)} %bitcast.501), channel_id=1, replica_groups=mesh['dp'=4,'expert'=8] {'dp','expert'}, dimensions={0}, use_global_device_ids=true | all-gather | bytes 12672 | tf_op jit(solution)/shard_map/all_gather | solution.py:100
  325.4 14.7 collective-permute-done.1
  467.4 14.1 all-to-all-done.4
  504.2 17.0 %all-to-all-done.5 = bf16[8,72,768]{2,1,0:T(8,128)(2,1)S(1)} async-done(((bf16[8,72,768]{2,1,0:T(8,128)(2,1)}), bf16[8,72,768]{2,1,0:T(8,128)(2,1)S(1)}, u32[]{:S(2)}, u32[]{:S(2)}) %all-to-all-start.5) | async-done | bytes 884768 | tf_op jit(solution)/shard_map/all_to_all | solution.py:239
  537.4 26.2 %all_to_all.40 = bf16[8,72,768]{2,1,0:T(8,128)(2,1)S(1)} all-to-all(bf16[8,72,768]{2,1,0:T(8,128)(2,1)S(1)} %bitcast.410), channel_id=1, replica_groups=mesh['dp'=4,'expert'=8] {'expert'}, dimensions={0} | all-to-all | bytes 1769472 | tf_op jit(solution)/shard_map/all_to_all | solution.py:184
  585.2 15.5 all-to-all-done.3
  623.9 17.1 %all-to-all-done.6 = bf16[8,72,768]{2,1,0:T(8,128)(2,1)S(1)} async-done(((bf16[8,72,768]{2,1,0:T(8,128)(2,1)}), bf16[8,72,768]{2,1,0:T(8,128)(2,1)S(1)}, u32[]{:S(2)}, u32[]{:S(2)}) %all-to-all-start.6) | async-done | bytes 884768 | tf_op jit(solution)/shard_map/all_to_all | solution.py:224
  662.8 11.9 fusion.176
  767.9 23.2 %rev.42 = f32[4,256,1024]{2,1,0:T(8,128)} reverse(bf16[4,256,1024]{2,1,0:T(8,128)(2,1)S(1)} %multiply_convert_fusion.5), dimensions={2} | reverse | bytes 6291456 | tf_op jit(solution)/shard_map/jit(_flip)/rev | solution.py:285
  791.1 32.6 %rev.41 = f32[4,256,1024]{2,1,0:T(8,128)} reverse(bf16[4,256,1024]{2,1,0:T(8,128)(2,1)} %copy-done.23), dimensions={2} | reverse | bytes 6291456 | tf_op jit(solution)/shard_map/jit(_flip)/rev | solution.py:285
  823.7 23.2 %rev.40 = f32[4,256,1024]{2,1,0:T(8,128)} reverse(bf16[4,256,1024]{2,1,0:T(8,128)(2,1)S(1)} %copy-done.25), dimensions={2} | reverse | bytes 6291456 | tf_op jit(solution)/shard_map/jit(_flip)/rev | solution.py:285
  846.9 32.4 %rev.45 = f32[4,256,1024]{2,1,0:T(8,128)} reverse(bf16[4,256,1024]{2,1,0:T(8,128)(2,1)} %copy-done.26), dimensions={2} | reverse | bytes 6291456 | tf_op jit(solution)/shard_map/jit(_flip)/rev | solution.py:285
  885.4 23.2 %rev.44 = f32[4,256,1024]{2,1,0:T(8,128)} reverse(bf16[4,256,1024]{2,1,0:T(8,128)(2,1)S(1)} %multiply_convert_fusion.3), dimensions={2} | reverse | bytes 6291456 | tf_op jit(solution)/shard_map/jit(_flip)/rev | solution.py:285
  914.4 23.2 %rev.43 = f32[4,256,1024]{2,1,0:T(8,128)} reverse(bf16[4,256,1024]{2,1,0:T(8,128)(2,1)S(1)} %multiply_convert_fusion.4), dimensions={2} | reverse | bytes 6291456 | tf_op jit(solution)/shard_map/jit(_flip)/rev | solution.py:285
  1126.1 12.9 fusion.31
  1168.5 84.3 %all-reduce.27.cloned.1.call-done = (f32[1024,12]{0,1:T(8,128)}, f32[768]{0:T(1024)}, f32[768]{0:T(1024)}, f32[768,8]{0,1:T(8,128)}) async-done(((f32[1024,12]{0,1:T(8,128)}, f32[768]{0:T(1024)}, f32[768]{0:T(1024)}, f32[768,8]{0,1:T(8,128)}), (f32[1024,12]{0,1:T(8,128)}, f32[768]{0:T(1024)}, f32[768]{0:T(1024)}, f32[768,8]{0,1:T(8,128)})) %all-reduce.27.cloned.1.call-update) | async-done | bytes 79888 | tf_op jit(solution)/shard_map/psum | solution.py:339
  1256.8 47.3 %reduce-scatter.12.cloned.1.call-done = bf16[1,768,768]{2,1,0:T(8,128)(2,1)} async-done(((bf16[1,3072,768]{2,1,0:T(8,128)(2,1)}), bf16[1,768,768]{2,1,0:T(8,128)(2,1)}) %reduce-scatter.12.cloned.1.call-update) | async-done | bytes 1179664 | tf_op jit(solution)/shard_map/reduce_scatter | solution.py:335
  1306.9 47.6 %reduce-scatter.10.cloned.1.call-done = bf16[1,192,3072]{2,1,0:T(8,128)(2,1)} async-done(((bf16[1,768,3072]{2,1,0:T(8,128)(2,1)}), bf16[1,192,3072]{2,1,0:T(8,128)(2,1)}) %reduce-scatter.10.cloned.1.call-update) | async-done | bytes 1179664 | tf_op jit(solution)/shard_map/reduce_scatter | solution.py:332
  1357.4 101.8 %reduce-scatter.8.cloned.1.call-done = f32[24,768]{1,0:T(8,128)} async-done(((f32[768,768]{1,0:T(8,128)}), f32[24,768]{1,0:T(8,128)}) %reduce-scatter.8.cloned.1.call-update) | async-done | bytes 73744 | tf_op jit(solution)/shard_map/reduce_scatter | solution.py:326
  1459.3 125.3 %reduce-scatter.6.cloned.1.call-done = f32[24,2304]{1,0:T(8,128)} async-done(((f32[768,2304]{1,0:T(8,128)}), f32[24,2304]{1,0:T(8,128)}) %reduce-scatter.6.cloned.1.call-update) | async-done | bytes 221200 | tf_op jit(solution)/shard_map/reduce_scatter | solution.py:325
  (764 shorter events, 668.7 us)
Async XLA Ops:
  7.2 293.4 %all-gather.4.cloned.1.call-start = ((), (), s32[]{:S(2)}) async-start(), calls=%async_computation.12 | async-start | bytes 3649536 | tf_op jit(solution)/shard_map/all_gather | solution.py:98
  7.9 362.0 %all-gather.6.cloned.1.call-start = ((), (), s32[]{:S(2)}) async-start(), calls=%async_computation.13 | async-start | bytes 1216512 | tf_op jit(solution)/shard_map/all_gather | solution.py:99
  305.3 34.8 %collective-permute-start.1 = (bf16[256,1536]{1,0:T(8,128)(2,1)S(1)}, bf16[256,1536]{1,0:T(8,128)(2,1)}, u32[]{:S(2)}, u32[]{:S(2)}) collective-permute-start(bf16[256,1536]{1,0:T(8,128)(2,1)S(1)} %slice.294), channel_id=1, source_target_pairs={{0,16},{8,24},{1,17},{9,25},{2,18},{10,26},{3,19},{11,27},{4,20},{... | collective-permute-start | bytes 2359304 | tf_op jit(solution)/shard_map/ppermute | solution.py:20
  308.0 32.1 %collective-permute-start.2 = (bf16[256,1536]{1,0:T(8,128)(2,1)S(1)}, bf16[256,1536]{1,0:T(8,128)(2,1)}, u32[]{:S(2)}, u32[]{:S(2)}) collective-permute-start(bf16[256,1536]{1,0:T(8,128)(2,1)S(1)} %slice.294), channel_id=1, source_target_pairs={{0,8},{8,16},{16,24},{1,9},{9,17},{17,25},{2,10},{10,18},{18,26},{... | collective-permute-start | bytes 2359304 | tf_op jit(solution)/shard_map/ppermute | solution.py:20
  312.4 67.5 %collective-permute-start.3 = (bf16[256,1536]{1,0:T(8,128)(2,1)}, bf16[256,1536]{1,0:T(8,128)(2,1)}, u32[]{:S(2)}, u32[]{:S(2)}) collective-permute-start(bf16[256,1536]{1,0:T(8,128)(2,1)} %slice.307), channel_id=1, source_target_pairs={{0,24},{1,25},{2,26},{3,27},{4,28},{5,29},{6,30},{7,31}} | collective-permute-start | bytes 2359304 | tf_op jit(solution)/shard_map/ppermute | solution.py:20
  314.6 65.3 %collective-permute-start.4 = (bf16[256,1536]{1,0:T(8,128)(2,1)}, bf16[256,1536]{1,0:T(8,128)(2,1)}, u32[]{:S(2)}, u32[]{:S(2)}) collective-permute-start(bf16[256,1536]{1,0:T(8,128)(2,1)} %slice.307), channel_id=1, source_target_pairs={{0,16},{8,24},{1,17},{9,25},{2,18},{10,26},{3,19},{11,27},{4,20},{... | collective-permute-start | bytes 2359304 | tf_op jit(solution)/shard_map/ppermute | solution.py:20
  323.2 56.7 %collective-permute-start.5 = (bf16[256,1536]{1,0:T(8,128)(2,1)}, bf16[256,1536]{1,0:T(8,128)(2,1)}, u32[]{:S(2)}, u32[]{:S(2)}) collective-permute-start(bf16[256,1536]{1,0:T(8,128)(2,1)} %slice.307), channel_id=1, source_target_pairs={{0,8},{8,16},{16,24},{1,9},{9,17},{17,25},{2,10},{10,18},{18,26},{... | collective-permute-start | bytes 2359304 | tf_op jit(solution)/shard_map/ppermute | solution.py:20
  416.1 26.5 %all-to-all-start.1 = ((bf16[8,72,768]{2,1,0:T(8,128)(2,1)}), bf16[8,72,768]{2,1,0:T(8,128)(2,1)}, u32[]{:S(2)}, u32[]{:S(2)}) async-start(bf16[8,72,768]{2,1,0:T(8,128)(2,1)} %bitcast.459), calls=%async_computation.1 | async-start | bytes 1769472 | tf_op jit(solution)/shard_map/all_to_all | solution.py:192
  455.0 26.5 %all-to-all-start.4 = ((bf16[8,72,768]{2,1,0:T(8,128)(2,1)}), bf16[8,72,768]{2,1,0:T(8,128)(2,1)}, u32[]{:S(2)}, u32[]{:S(2)}) async-start(bf16[8,72,768]{2,1,0:T(8,128)(2,1)} %bitcast.74), calls=%async_computation.4 | async-start | bytes 1769472 | tf_op jit(solution)/shard_map/all_to_all | solution.py:224
  495.2 26.1 %all-to-all-start.5 = ((bf16[8,72,768]{2,1,0:T(8,128)(2,1)}), bf16[8,72,768]{2,1,0:T(8,128)(2,1)S(1)}, u32[]{:S(2)}, u32[]{:S(2)}) async-start(bf16[8,72,768]{2,1,0:T(8,128)(2,1)} %bitcast.461), calls=%async_computation.5 | async-start | bytes 1769472 | tf_op jit(solution)/shard_map/all_to_all | solution.py:239
  574.8 26.0 %all-to-all-start.3 = ((bf16[8,72,768]{2,1,0:T(8,128)(2,1)}), bf16[8,72,768]{2,1,0:T(8,128)(2,1)}, u32[]{:S(2)}, u32[]{:S(2)}) async-start(bf16[8,72,768]{2,1,0:T(8,128)(2,1)} %bitcast.60), calls=%async_computation.3 | async-start | bytes 1769472 | tf_op jit(solution)/shard_map/all_to_all | solution.py:192
  614.6 26.4 %all-to-all-start.6 = ((bf16[8,72,768]{2,1,0:T(8,128)(2,1)}), bf16[8,72,768]{2,1,0:T(8,128)(2,1)S(1)}, u32[]{:S(2)}, u32[]{:S(2)}) async-start(bf16[8,72,768]{2,1,0:T(8,128)(2,1)} %bitcast.409), calls=%async_computation.6 | async-start | bytes 1769472 | tf_op jit(solution)/shard_map/all_to_all | solution.py:224
  659.0 26.0 %all-to-all-start.7 = ((bf16[8,72,768]{2,1,0:T(8,128)(2,1)}), bf16[8,72,768]{2,1,0:T(8,128)(2,1)S(1)}, u32[]{:S(2)}, u32[]{:S(2)}) async-start(bf16[8,72,768]{2,1,0:T(8,128)(2,1)} %bitcast.460), calls=%async_computation.7 | async-start | bytes 1769472 | tf_op jit(solution)/shard_map/all_to_all | solution.py:239
  662.6 590.3 %all-reduce.27.cloned.1.call-start = ((), (), s32[]{:S(2)}) async-start(), calls=%async_computation.18 | async-start | bytes 196608 | tf_op jit(solution)/shard_map/psum | solution.py:339
  944.7 33.4 %collective-permute-start.6 = (bf16[256,1536]{0,1:T(8,128)(2,1)S(1)}, bf16[256,1536]{0,1:T(8,128)(2,1)S(1)}, u32[]{:S(2)}, u32[]{:S(2)}) collective-permute-start(bf16[256,1536]{0,1:T(8,128)(2,1)S(1)} %get-tuple-element.76), channel_id=1, source_target_pairs={{8,0},{16,8},{24,16},{9,1},{17,9},{25,17},{10,2},{18,10},{26,18},{... | collective-permute-start | bytes 2359304 | tf_op jit(solution)/shard_map/ppermute | solution.py:20
  946.2 170.4 %collective-permute-start.7 = (bf16[256,1536]{0,1:T(8,128)(2,1)}, bf16[256,1536]{0,1:T(8,128)(2,1)}, u32[]{:S(2)}, u32[]{:S(2)}) collective-permute-start(bf16[256,1536]{0,1:T(8,128)(2,1)} %get-tuple-element.78), channel_id=1, source_target_pairs={{16,0},{24,8},{17,1},{25,9},{18,2},{26,10},{19,3},{27,11},{20,4},{... | collective-permute-start | bytes 2359304 | tf_op jit(solution)/shard_map/ppermute | solution.py:20
  947.5 169.1 %collective-permute-start.8 = (bf16[256,1536]{0,1:T(8,128)(2,1)}, bf16[256,1536]{0,1:T(8,128)(2,1)}, u32[]{:S(2)}, u32[]{:S(2)}) collective-permute-start(bf16[256,1536]{0,1:T(8,128)(2,1)} %get-tuple-element.77), channel_id=1, source_target_pairs={{24,0},{25,1},{26,2},{27,3},{28,4},{29,5},{30,6},{31,7}} | collective-permute-start | bytes 2359304 | tf_op jit(solution)/shard_map/ppermute | solution.py:20
  954.7 164.2 %collective-permute-start.10 = (bf16[256,1536]{0,1:T(8,128)(2,1)}, bf16[256,1536]{0,1:T(8,128)(2,1)}, u32[]{:S(2)}, u32[]{:S(2)}) collective-permute-start(bf16[256,1536]{0,1:T(8,128)(2,1)} %get-tuple-element.81), channel_id=1, source_target_pairs={{16,0},{24,8},{17,1},{25,9},{18,2},{26,10},{19,3},{27,11},{20,4},{... | collective-permute-start | bytes 2359304 | tf_op jit(solution)/shard_map/ppermute | solution.py:20
  956.1 162.8 %collective-permute-start.11 = (bf16[256,1536]{0,1:T(8,128)(2,1)}, bf16[256,1536]{0,1:T(8,128)(2,1)}, u32[]{:S(2)}, u32[]{:S(2)}) collective-permute-start(bf16[256,1536]{0,1:T(8,128)(2,1)} %get-tuple-element.80), channel_id=1, source_target_pairs={{24,0},{25,1},{26,2},{27,3},{28,4},{29,5},{30,6},{31,7}} | collective-permute-start | bytes 2359304 | tf_op jit(solution)/shard_map/ppermute | solution.py:20
  978.2 140.8 %collective-permute-start.9 = (bf16[256,1536]{0,1:T(8,128)(2,1)}, bf16[256,1536]{0,1:T(8,128)(2,1)}, u32[]{:S(2)}, u32[]{:S(2)}) collective-permute-start(bf16[256,1536]{0,1:T(8,128)(2,1)} %get-tuple-element.79), channel_id=1, source_target_pairs={{8,0},{16,8},{24,16},{9,1},{17,9},{25,17},{10,2},{18,10},{26,18},{... | collective-permute-start | bytes 2359304 | tf_op jit(solution)/shard_map/ppermute | solution.py:20
  1125.8 178.2 %reduce-scatter.12.cloned.1.call-start = ((), (), s32[]{:S(2)}) async-start(), calls=%async_computation.17 | async-start | bytes 5898240 | tf_op jit(solution)/shard_map/reduce_scatter | solution.py:335
  1139.0 215.5 %reduce-scatter.10.cloned.1.call-start = ((), (), s32[]{:S(2)}) async-start(), calls=%async_computation.16 | async-start | bytes 5898240 | tf_op jit(solution)/shard_map/reduce_scatter | solution.py:332
  1151.0 308.2 %reduce-scatter.8.cloned.1.call-start = ((), (), s32[]{:S(2)}) async-start(), calls=%async_computation.15 | async-start | bytes 2433024 | tf_op jit(solution)/shard_map/reduce_scatter | solution.py:326
  1156.6 428.0 %reduce-scatter.6.cloned.1.call-start = ((), (), s32[]{:S(2)}) async-start(), calls=%async_computation.14 | async-start | bytes 7299072 | tf_op jit(solution)/shard_map/reduce_scatter | solution.py:325
  (215 other events, 3455.6 us)
Sparse Core Ops, SparseCore 0:
  11.0 62.9 all-gather.3
  77.0 52.9 all-gather.5
  1126.0 126.8 all-reduce.26
  1255.3 48.7 reduce-scatter.11
  1306.6 47.8 reduce-scatter.9
  1360.2 99.0 reduce-scatter.7
  1466.5 118.0 reduce-scatter.5
where the time goes:
time: 1620 us; the launch traced here: 1590 us
  local copies, waits for them, and re-layouts  569 us (35%)
  waiting for transfers between devices  504 us (31%)
  matrix products  221 us (14%)
  blocking collectives  135 us (8%)
  other arithmetic  94.1 us (6%)
  starting transfers between devices  52.1 us (3%)
  between operations  17.5 us (1%)
    rev x6, local copies, waits for them, and re-layouts, shards(): jnp.flip(score_grad.astype(jnp.float32), axis=-1)  158 us
    reduce_scatter x1, waiting for transfers between devices, shards(): lax.psum_scatter(grad_qkv, ('dp', 'expert'), scatter_dimension=0, tiled=T...  125 us
    rev x3, local copies, waits for them, and re-layouts, group_scores(): jnp.flip(shear_band(band_all[start_head:start_head + 4], tok_rows, key_co...  104 us
    reduce_scatter x1, waiting for transfers between devices, shards(): lax.psum_scatter(grad_out, ('dp', 'expert'), scatter_dimension=0, tiled=T...  102 us
    unnamed x460, local copies, waits for them, and re-layouts  90.9 us
    psum x1, waiting for transfers between devices, shards(): lax.psum(band_grad[:, tok_rows - 1:tok_rows - 1 + WINDOW].T, ('dp', 'expe...  84.3 us
    reshape x6, local copies, waits for them, and re-layouts, unshear(): return jnp.sum(flattened.reshape(leading + (height, extent)), axis=-2)  67.2 us
    all_gather x1, blocking collectives, collect_dense(): lax.all_gather(w_router, ('dp', 'expert'), axis=0, tiled=True)  66.3 us
  transfers between devices with their start and end apart: 26, of which 14 were waited for; matrix products, arithmetic and copies ran while one was open for 31% of the time, Pallas kernels for 0%

commit v1 on v0

v1 whole, which is shorter than its diff:
```python
import functools

import jax
import jax.numpy as jnp
from jax import lax
from jax.experimental import pallas as pl
from jax.experimental.pallas import tpu as pltpu
from jax.sharding import PartitionSpec as P

H = 12
HD = 64
TOP = 2
WINDOW = 1024
EPSILON = 1e-06
MASKED = -1e30
LANES = 128

bf16 = jnp.bfloat16
f32 = jnp.float32
MIB = 1 << 20

NN = (((1,), (0,)), ((), ()))
NT = (((1,), (1,)), ((), ()))
TN = (((0,), (0,)), ((), ()))


def dot(a, b, dims=NN):
    return lax.dot_general(a, b, dims, preferred_element_type=f32)


def rsq(x):
    return lax.rsqrt(jnp.mean(x * x, axis=-1, keepdims=True) + EPSILON)


def call(kernel, outs, name, flops=0, scratch=(), n_smem=0, n_in=0, limit=48, trans=0, bytes_accessed=4 * MIB):
    smem = pl.BlockSpec(memory_space=pltpu.SMEM)
    vmem = pl.BlockSpec(memory_space=pltpu.VMEM)
    return pl.pallas_call(
        kernel,
        out_shape=[jax.ShapeDtypeStruct(s, d) for s, d in outs],
        in_specs=[smem] * n_smem + [vmem] * n_in,
        out_specs=[vmem] * len(outs),
        scratch_shapes=list(scratch),
        compiler_params=pltpu.CompilerParams(vmem_limit_bytes=limit * MIB),
        cost_estimate=pl.CostEstimate(
            flops=int(flops), transcendentals=int(trans), bytes_accessed=int(bytes_accessed)
        ),
        name=name,
    )


def tiles_kernel(spans, rows, band_ref, out_ref):
    heads = out_ref.shape[0]
    for h in range(heads):
        for s in range(spans):
            ahead = band_ref[h : h + 1, (s + 1) * rows : (s + 2) * rows]
            behind = band_ref[h : h + 1, s * rows : (s + 1) * rows]
            line = jnp.concatenate([ahead, behind], axis=1)
            spread = jnp.broadcast_to(line, (rows, 2 * rows))
            rolled = pltpu.roll(spread, 0, axis=1, stride=1, stride_axis=0)
            out_ref[h, s] = rolled[:, :rows]


def dispatch_cot_kernel(places_ref, other_ref, cot_ref, rows_ref, ids_ref):
    micros, _, tok = places_ref.shape
    total = rows_ref.shape[0]
    width = cot_ref.shape[-1]
    slot = lax.broadcasted_iota(jnp.int32, (total, tok), 0)
    for m in range(micros):
        picks = None
        ids = None
        for k in range(TOP):
            hit = slot == places_ref[m, k : k + 1, :]
            one = jnp.where(hit, 1.0, 0.0)
            other = jnp.sum(
                jnp.where(hit, other_ref[m, k : k + 1, :].astype(f32), 0.0),
                axis=1,
                keepdims=True,
            )
            picks = one if picks is None else picks + one
            ids = other if ids is None else ids + other
        rows_ref[:, m * width : (m + 1) * width] = dot(picks.astype(bf16), cot_ref[m]).astype(bf16)
        ids_ref[:, m : m + 1] = ids.astype(jnp.int32)


def attn_fwd_kernel(m, n, reach, heads, idx_ref, gain_ref, w_ref, tiles_ref, kdoc_ref, qdoc_ref, *rest):
    x_refs = rest[:n]
    att_ref, qkv_ref, lse_ref, vt_scr, ot_scr = rest[n:]
    tok = x_refs[0].shape[1]
    groups = qkv_ref.shape[0] // 3
    me = idx_ref[0]
    gain = gain_ref[...]
    for r in range(n):
        start = pl.multiple_of(jnp.bitwise_xor(me, r) * tok, tok)
        x = x_refs[r][m].astype(f32)
        normed = (x * rsq(x) * gain).astype(bf16)
        qkv = dot(normed, w_ref[...]).astype(bf16)
        for c in range(3 * groups):
            qkv_ref[c, pl.ds(start, tok), :] = qkv[:, c * LANES : (c + 1) * LANES]
    for g in range(groups):
        vt_scr[g * LANES : (g + 1) * LANES, :] = qkv_ref[2 * groups + g].astype(f32).T.astype(bf16)
    lse_ref[...] = jnp.zeros_like(lse_ref)

    def head_body(h, carry):
        g = lax.shift_right_logical(h, 1)
        half = jnp.bitwise_and(h, 1)
        lane = lax.broadcasted_iota(jnp.int32, (tok, LANES), 1)
        mine = lax.shift_right_logical(lane, 6) == half
        for j in range(n):
            lo = max(0, j - reach)
            q = qkv_ref[g, j * tok : (j + 1) * tok, :].astype(f32)
            q = jnp.where(mine, q * HD ** (-0.5), 0.0).astype(bf16)
            key = qkv_ref[groups + g, lo * tok : (j + 1) * tok, :]
            s = dot(key, q, NT)
            bias = jnp.concatenate([tiles_ref[h, j - b] for b in range(lo, j + 1)], axis=0)
            ok = kdoc_ref[lo * tok : (j + 1) * tok, :] == qdoc_ref[:, j * tok : (j + 1) * tok]
            s = jnp.where(ok, s + bias, MASKED)
            peak = jnp.max(s, axis=0, keepdims=True)
            e = jnp.exp(s - peak)
            total = jnp.sum(e, axis=0, keepdims=True)
            p = (e * (1.0 / total)).astype(bf16)
            lse_ref[pl.ds(h, 1), j * tok : (j + 1) * tok] = peak + jnp.log(total)
            vt = vt_scr[pl.ds(pl.multiple_of(h * HD, HD), HD), lo * tok : (j + 1) * tok]
            ot_scr[pl.ds(pl.multiple_of(h * HD, HD), HD), j * tok : (j + 1) * tok] = dot(vt, p)
        return carry

    lax.fori_loop(0, heads, head_body, 0)
    att_ref[...] = ot_scr[...].T[:, : heads * HD].astype(bf16)


def unshear_rows(tile):
    rows = tile.shape[0]
    wide = jnp.concatenate([tile, jnp.zeros_like(tile)], axis=1)
    span = 2 * rows
    count = rows
    while count > 1:
        count //= 2
        wide = wide[:count] + pltpu.roll(wide[count : 2 * count], span - count, axis=1)
    return wide


def attn_bwd_kernel(
    m, n, reach, heads, first, idx_ref, gain_ref, w_ref, tiles_ref, kdoc_ref, qdoc_ref, qkv_ref, lse_ref, grad_ref, *rest
):
    x_refs = rest[:n]
    rest = rest[n:]
    if not first:
        old_w_ref, old_small_ref, old_band_ref = rest[:3]
        rest = rest[3:]
    part_refs = rest[:n]
    new_w_ref, new_small_ref, new_band_ref, normed_scr, da_scr, kt_scr, dqt_scr, dkv_scr, dqkv_scr, acc_scr = rest[n:]
    tok = x_refs[0].shape[1]
    groups = qkv_ref.shape[0] // 3
    spans = tiles_ref.shape[1]
    wide = groups * LANES
    me = idx_ref[0]
    gain = gain_ref[...]
    for r in range(n):
        start = pl.multiple_of(jnp.bitwise_xor(me, r) * tok, tok)
        x = x_refs[r][m].astype(f32)
        normed_scr[pl.ds(start, tok), :] = (x * rsq(x) * gain).astype(bf16)
    if heads * HD < wide:
        da_scr[...] = jnp.zeros_like(da_scr)
    for d in range(n):
        for g in range(groups):
            cols = min(LANES, heads * HD - g * LANES)
            da_scr[g, d * tok : (d + 1) * tok, :cols] = grad_ref[d, :, g * LANES : g * LANES + cols]
    for g in range(groups):
        kt_scr[g * LANES : (g + 1) * LANES, :] = qkv_ref[groups + g].astype(f32).T.astype(bf16)
    dkv_scr[...] = jnp.zeros_like(dkv_scr)
    dqt_scr[...] = jnp.zeros_like(dqt_scr)
    acc_scr[...] = jnp.zeros_like(acc_scr)

    def head_body(h, carry):
        g = lax.shift_right_logical(h, 1)
        half = jnp.bitwise_and(h, 1)
        lane = lax.broadcasted_iota(jnp.int32, (tok, LANES), 1)
        mine = lax.shift_right_logical(lane, 6) == half
        for j in range(n):
            lo = max(0, j - reach)
            rows = slice(lo * tok, (j + 1) * tok)
            cols = slice(j * tok, (j + 1) * tok)
            q = qkv_ref[g, cols, :].astype(f32)
            q = jnp.where(mine, q * HD ** (-0.5), 0.0).astype(bf16)
            da = jnp.where(mine, da_scr[g, cols, :].astype(f32), 0.0).astype(bf16)
            s = dot(qkv_ref[groups + g, rows, :], q, NT)
            bias = jnp.concatenate([tiles_ref[h, j - b] for b in range(lo, j + 1)], axis=0)
            ok = kdoc_ref[rows, :] == qdoc_ref[:, cols]
            s = jnp.where(ok, s + bias, MASKED)
            p = jnp.exp(s - lse_ref[pl.ds(h, 1), cols])
            pg = dot(qkv_ref[2 * groups + g, rows, :], da, NT)
            centre = jnp.sum(p * pg, axis=0, keepdims=True)
            sg = (p * (pg - centre)).astype(bf16)
            for b in range(lo, j + 1):
                acc_scr[h, j - b] += sg[(b - lo) * tok : (b - lo + 1) * tok].astype(f32)
            dkv_scr[g, rows, :] += dot(sg, q)
            dkv_scr[groups + g, rows, :] += dot(p.astype(bf16), da)
            at = pl.ds(pl.multiple_of(h * HD, HD), HD)
            dqt_scr[at, cols] = dot(kt_scr[at, rows], sg) * HD ** (-0.5)
        return carry

    lax.fori_loop(0, heads, head_body, 0)
    for g in range(groups):
        dqkv_scr[:, g * LANES : (g + 1) * LANES] = dqt_scr[g * LANES : (g + 1) * LANES, :].T.astype(bf16)
    for c in range(2 * groups):
        dqkv_scr[:, wide + c * LANES : wide + (c + 1) * LANES] = dkv_scr[c].astype(bf16)
    small = None
    for r in range(n):
        start = pl.multiple_of(jnp.bitwise_xor(me, r) * tok, tok)
        x = x_refs[r][m].astype(f32)
        part = dot(dqkv_scr[pl.ds(start, tok), :], w_ref[...], NT)
        part_refs[r][...] = part.astype(bf16)
        term = jnp.sum(part * (x * rsq(x)), axis=0, keepdims=True)
        small = term if small is None else small + term
    new_w = dot(normed_scr[...], dqkv_scr[...], TN)
    if not first:
        new_w = new_w + old_w_ref[...]
        small = small + old_small_ref[0:1, :]
    new_w_ref[...] = new_w.astype(new_w_ref.dtype)
    new_small_ref[...] = jnp.broadcast_to(small, new_small_ref.shape)
    new_band_ref[...] = jnp.zeros_like(new_band_ref)
    for h in range(heads):
        lines = [unshear_rows(acc_scr[h, s]) for s in range(spans)]
        for s in range(spans):
            value = lines[s][:, :tok]
            if s + 1 < spans:
                value = value + lines[s + 1][:, tok:]
            if not first:
                value = value + old_band_ref[h : h + 1, s * tok : (s + 1) * tok]
            new_band_ref[h : h + 1, s * tok : (s + 1) * tok] = value


def mid_kernel(m, heads, x_ref, att_ref, dense_ref, gain_ref, places_ref, mixed_ref, rows_ref):
    n, tok, part = att_ref.shape
    width = x_ref.shape[-1]
    total = rows_ref.shape[0]
    mixed = x_ref[m].astype(f32)
    for d in range(n):
        size = min(part, width - d * part)
        if size > 0:
            mixed = mixed + dot(att_ref[d][:, :size], dense_ref[d * part : d * part + size, :width])
    mixed_ref[...] = mixed
    normed = (mixed * rsq(mixed) * gain_ref[...]).astype(bf16)
    slot = lax.broadcasted_iota(jnp.int32, (total, tok), 0)
    picks = jnp.where(slot == places_ref[m, 0:1, :], 1.0, 0.0)
    picks = picks + jnp.where(slot == places_ref[m, 1:2, :], 1.0, 0.0)
    rows_ref[...] = dot(picks.astype(bf16), normed).astype(bf16)


def expert_kernel(m, e_ref, x_ref, c_ref, ids_ref, dense_ref, win_ref, wback_ref, out_ref, hid_ref, pre_ref, g_ref, acc_scr, grad_scr):
    f = pl.program_id(0)
    width = x_ref.shape[-1]

    @pl.when(f == 0)
    def _():
        logits = dot(x_ref[...], dense_ref[...])
        lane = lax.broadcasted_iota(jnp.int32, logits.shape, 1)
        own = jnp.sum(jnp.where(lane == e_ref[0], logits, 0.0), axis=1, keepdims=True)
        other = jnp.sum(jnp.where(lane == ids_ref[:, m : m + 1], logits, 0.0), axis=1, keepdims=True)
        peak = jnp.maximum(own, other)
        own = jnp.exp(own - peak)
        gate = own / (own + jnp.exp(other - peak))
        grad = (gate * c_ref[...].astype(f32)).astype(bf16)
        grad_scr[...] = grad
        g_ref[...] = grad
        acc_scr[...] = jnp.zeros_like(acc_scr)

    pre = dot(x_ref[...], win_ref[...])
    c0 = 0.7978845608028654
    square = pre * pre
    t = jnp.tanh(pre * (c0 + (c0 * 0.044715) * square))
    hidden = (0.5 * pre * (1.0 + t)).astype(bf16)
    hid_ref[...] = hidden
    slope = 0.5 * (1.0 + t) + 0.5 * pre * (1.0 - t * t) * (c0 + (3 * c0 * 0.044715) * square)
    acc_scr[:, :width] += dot(hidden, wback_ref[...])
    pre_grad = (dot(grad_scr[...], wback_ref[...], NT) * slope).astype(bf16)
    pre_ref[...] = pre_grad
    acc_scr[:, width:] += dot(pre_grad, win_ref[...], NT)

    @pl.when(f == pl.num_programs(0) - 1)
    def _():
        out_ref[...] = acc_scr[...].astype(bf16)


def grad_back_kernel(pos_ref, h0_ref, h1_ref, g0_ref, g1_ref, out_ref):
    out_ref[...] = (dot(h0_ref[...], g0_ref[...], TN) + dot(h1_ref[...], g1_ref[...], TN)).astype(bf16)


def grad_in_kernel(pos_ref, x0_ref, x1_ref, p0_ref, p1_ref, out_ref):
    value = (dot(x0_ref[...], p0_ref[...], TN) + dot(x1_ref[...], p1_ref[...], TN)).astype(bf16)
    n, rows, _ = out_ref.shape
    for b in range(n):
        out_ref[pos_ref[b]] = value[b * rows : (b + 1) * rows]


def combine_kernel(m, first, back_ref, places_ref, routes_ref, mixed_ref, cot_ref, att_ref, dense_ref, gain_ref, *rest):
    if not first:
        old_ref = rest[0]
        rest = rest[1:]
    out_ref, da_ref, mg_ref, new_ref = rest
    n, tok, part = att_ref.shape
    width = mixed_ref.shape[-1]
    total = back_ref.shape[0]
    mixed = mixed_ref[...]
    gain = gain_ref[...]
    rr = rsq(mixed)
    normed = (mixed * rr * gain).astype(bf16)
    router = dense_ref[:, width:]
    logits = dot(normed, router)
    lane = lax.broadcasted_iota(jnp.int32, logits.shape, 1)
    route = [lane == routes_ref[m, :, k : k + 1] for k in range(TOP)]
    chosen = [jnp.sum(jnp.where(r, logits, 0.0), axis=1, keepdims=True) for r in route]
    peak = jnp.maximum(chosen[0], chosen[1])
    powers = [jnp.exp(c - peak) for c in chosen]
    whole = powers[0] + powers[1]
    gates = [v / whole for v in powers]
    slot = lax.broadcasted_iota(jnp.int32, (tok, total), 1)
    hits = [jnp.where(slot == places_ref[m, :, k : k + 1], 1.0, 0.0) for k in range(TOP)]
    results = back_ref[:, :width]
    returned = [dot(h.astype(bf16), results) for h in hits]
    moe = gates[0] * returned[0] + gates[1] * returned[1]
    out_ref[...] = (mixed + moe).astype(bf16)
    up = cot_ref[m].astype(f32)
    gate_grad = [jnp.sum(up * v, axis=1, keepdims=True) for v in returned]
    centre = gates[0] * gate_grad[0] + gates[1] * gate_grad[1]
    chosen_grad = [gates[k] * (gate_grad[k] - centre) for k in range(TOP)]
    logit_grad = jnp.where(route[0], chosen_grad[0], 0.0) + jnp.where(route[1], chosen_grad[1], 0.0)
    high = logit_grad.astype(bf16)
    low = (logit_grad - high.astype(f32)).astype(bf16)
    normed_grad = dot((hits[0] + hits[1]).astype(bf16), back_ref[:, width:])
    normed_grad = normed_grad + dot(high, router, NT) + dot(low, router, NT)
    router_grad = dot(normed, high, TN) + dot(normed, low, TN)
    scaled = mixed * rr
    gain_part = jnp.sum(normed_grad * scaled, axis=0, keepdims=True)
    ng = gain * normed_grad
    mixed_grad = up + rr * (ng - scaled * jnp.mean(ng * scaled, axis=-1, keepdims=True))
    mg_ref[...] = mixed_grad
    branch = mixed_grad.astype(bf16)
    gain_col = jnp.broadcast_to(gain_part, (LANES, width)).T
    lane = lax.broadcasted_iota(jnp.int32, gain_col.shape, 1)
    extra = jnp.where(lane == LANES - 1, gain_col, router_grad)
    if not first:
        extra = extra + old_ref[:, width:].astype(f32)
    new_ref[:, width:] = extra.astype(new_ref.dtype)
    for d in range(n):
        size = min(part, width - d * part)
        if size <= 0:
            da_ref[d] = jnp.zeros((tok, part), bf16)
            continue
        at = slice(d * part, d * part + size)
        piece = dot(branch, dense_ref[at, :width], NT).astype(bf16)
        if size < part:
            piece = jnp.concatenate([piece, jnp.zeros((tok, part - size), bf16)], axis=1)
        da_ref[d] = piece
        grad = dot(att_ref[d][:, :size], branch, TN)
        if not first:
            grad = grad + old_ref[at, :width].astype(f32)
        new_ref[at, :width] = grad.astype(new_ref.dtype)


def token_grad_kernel(m, x_ref, mg_ref, gain_ref, *rest):
    parts, out_ref = rest[:-1], rest[-1]
    grad = parts[0][...].astype(f32)
    for p in parts[1:]:
        grad = grad + p[...].astype(f32)
    x = x_ref[m].astype(f32)
    r = rsq(x)
    scaled = x * r
    ng = gain_ref[...] * grad
    out_ref[...] = (
        mg_ref[...] + r * (ng - scaled * jnp.mean(ng * scaled, axis=-1, keepdims=True))
    ).astype(bf16)


def swap(x, axis, by):
    return lax.ppermute(x, axis, [(i, i ^ by) for i in range(lax.axis_size(axis))])


def exchange(x, axes):
    return lax.all_to_all(x, axes, split_axis=0, concat_axis=0, tiled=True)


def bit_reversed(n):
    bits = n.bit_length() - 1
    return [int(format(r, "b").zfill(bits)[::-1], 2) if bits else 0 for r in range(n)]


def halving_sum(x, axis):
    by = 1
    while x.shape[0] > 1:
        half = x.shape[0] // 2
        came = swap(x[half:], axis, by)
        x = x[:half].astype(f32) + came.astype(f32)
        if half > 1:
            x = x.astype(bf16)
        by *= 2
    return x[0]


def shards(
    tokens, doc_lengths, routes, slots, w_qkv, w_out, rel_bias, gain_attn, gain_ffn, w_router, w_in, w_back, cotangent
):
    micros, _, tok, width = tokens.shape
    n = lax.axis_size("dp")
    experts = lax.axis_size("expert")
    me = lax.axis_index("dp")
    my_expert = lax.axis_index("expert")
    reach = min((WINDOW - 2) // tok + 1, n - 1)
    spans = reach + 1
    capacity = (9 * tok * TOP + 8 * experts - 1) // (8 * experts)
    total = experts * capacity
    length = n * tok
    heads = -(-H // n)
    groups = -(-heads // 2)
    part = heads * HD
    wide = groups * LANES
    ff = w_in.shape[2]
    own_rows = w_qkv.shape[0]
    both = ("dp", "expert")
    tokens, cotangent = tokens[:, 0], cotangent[:, 0]
    routes, slots = routes[:, 0], slots[:, 0]
    idx = me.astype(jnp.int32).reshape(1)

    q_cols = w_qkv.reshape(own_rows, 3, H, HD)
    q_cols = jnp.pad(q_cols, ((0, 0), (0, 0), (0, heads * n - H), (0, 0)))
    q_cols = q_cols.reshape(own_rows, 3, n, part).transpose(2, 0, 1, 3).reshape(n, own_rows, 3 * part)
    send_cols = -(-(3 * part + 1) // LANES) * LANES
    gain_cols = jnp.broadcast_to(gain_attn[None, :, None], (n, own_rows, 1))
    q_cols = jnp.concatenate(
        [q_cols, gain_cols, jnp.zeros((n, own_rows, send_cols - 3 * part - 1), bf16)], axis=2
    )
    q_cols = jnp.broadcast_to(q_cols[:, None], (n, experts, own_rows, send_cols)).reshape(
        n * experts, own_rows, send_cols
    )
    w_mine = exchange(q_cols, both).reshape(width, send_cols)
    gain_a = w_mine[:, 3 * part].astype(f32)[None]
    w_heads = jnp.pad(
        w_mine[:, : 3 * part].reshape(width, 3, part), ((0, 0), (0, 0), (0, wide - part))
    ).reshape(width, 3 * wide)
    dense = jnp.concatenate(
        [
            w_out,
            w_router,
            jnp.zeros((own_rows, LANES - experts - 1), bf16),
            gain_ffn[:, None],
        ],
        axis=1,
    )
    dense = lax.all_gather(dense, both, axis=0, tiled=True)
    gain_f = dense[:, width + LANES - 1].astype(f32)[None]

    blocks = {0: tokens}
    by = n // 2
    while by:
        for r in list(blocks):
            blocks[r ^ by] = swap(blocks[r], "dp", by)
        by //= 2
    xs = [blocks[r] for r in range(n)]

    bias = jnp.pad(rel_bias.astype(f32).T, ((0, heads * n - H), (0, 0)))
    bias = lax.dynamic_slice_in_dim(bias, me * heads, heads, 0)[:, : spans * tok]
    band = jnp.concatenate(
        [
            jnp.full((heads, tok), MASKED, f32),
            bias,
            jnp.full((heads, spans * tok - bias.shape[1]), MASKED, f32),
        ],
        axis=1,
    )
    band = jnp.pad(band, ((0, -heads % 8), (0, 0)))
    (tiles,) = call(
        functools.partial(tiles_kernel, spans, tok),
        [((heads, spans, tok, tok), f32)],
        "bias_tiles",
        n_in=1,
    )(band)

    places = jnp.where(slots >= 0, routes * capacity + slots, total)
    places_row = places.transpose(0, 2, 1)
    other_row = routes[..., ::-1].transpose(0, 2, 1)
    doc_ends = jnp.cumsum(doc_lengths[:, 0], axis=-1)
    positions = jnp.arange(length, dtype=jnp.int32)
    docs = jnp.sum((doc_ends[:, None, :] <= positions[None, :, None]).astype(jnp.int32), axis=2)

    cot_rows, ids = call(
        dispatch_cot_kernel,
        [((total, micros * width), bf16), ((total, micros), jnp.int32)],
        "dispatch_cotangent",
        flops=2 * micros * total * tok * width,
        n_in=3,
    )(places_row, other_row, cotangent)
    ids = exchange(ids.reshape(experts, capacity, micros).transpose(0, 2, 1), "expert")
    ids = ids.transpose(0, 2, 1).reshape(total, micros)
    cot_rows, w_heads = lax.optimization_barrier((cot_rows, w_heads))
    cot_rows = exchange(cot_rows.reshape(experts, capacity, micros * width), "expert").reshape(
        total, micros * width
    )

    att = []
    saved = []
    pair_flops = 2 * heads * LANES * tok * tok * sum(min(j, reach) + 1 for j in range(n))
    for m in range(micros):
        kdoc, qdoc = docs[m][:, None], docs[m][None]
        att_m, qkv, lse = call(
            functools.partial(attn_fwd_kernel, m, n, reach, heads),
            [((length, part), bf16), ((3 * groups, length, LANES), bf16), ((8, length), f32)],
            "attention_forward",
            flops=2 * length * width * 3 * wide + 2 * pair_flops,
            scratch=[pltpu.VMEM((wide, length), bf16), pltpu.VMEM((wide, length), f32)],
            n_smem=1,
            n_in=5 + n,
        )(idx, gain_a, w_heads, tiles, kdoc, qdoc, *xs)
        att.append(exchange(att_m.reshape(n, tok, part), "dp"))
        saved.append((kdoc, qdoc, qkv, lse))

    mixed = []
    arrived = []
    for m in range(micros):
        mixed_m, rows = call(
            functools.partial(mid_kernel, m, heads),
            [((tok, width), f32), ((total, width), bf16)],
            "mix_and_dispatch",
            flops=2 * tok * width * width + 2 * total * tok * width,
            n_in=5,
        )(tokens, att[m], dense, gain_f, places_row)
        mixed.append(mixed_m)
        arrived.append(exchange(rows.reshape(experts, capacity, width), "expert").reshape(total, width))

    tile = 512
    back = []
    kept = []
    for m in range(micros):
        whole = lambda shape, c=0: pl.BlockSpec(shape, lambda f, c=c: (0, c))
        out, hid, pre, g = pl.pallas_call(
            functools.partial(expert_kernel, m),
            out_shape=[
                jax.ShapeDtypeStruct((total, 2 * width), bf16),
                jax.ShapeDtypeStruct((total, ff), bf16),
                jax.ShapeDtypeStruct((total, ff), bf16),
                jax.ShapeDtypeStruct((total, width), bf16),
            ],
            grid=(ff // tile,),
            in_specs=[
                pl.BlockSpec(memory_space=pltpu.SMEM),
                whole((total, width)),
                whole((total, width), m),
                whole((total, micros)),
                whole((width, LANES), width // LANES),
                pl.BlockSpec((None, width, tile), lambda f: (0, 0, f)),
                pl.BlockSpec((None, tile, width), lambda f: (0, f, 0)),
            ],
            out_specs=[
                whole((total, 2 * width)),
                pl.BlockSpec((total, tile), lambda f: (0, f)),
                pl.BlockSpec((total, tile), lambda f: (0, f)),
                whole((total, width)),
            ],
            scratch_shapes=[pltpu.VMEM((total, 2 * width), f32), pltpu.VMEM((total, width), bf16)],
            compiler_params=pltpu.CompilerParams(vmem_limit_bytes=48 * MIB),
            cost_estimate=pl.CostEstimate(
                flops=8 * total * width * ff, transcendentals=total * ff, bytes_accessed=20 * MIB
            ),
            name="expert",
        )(my_expert.astype(jnp.int32).reshape(1), arrived[m], cot_rows, ids, dense, w_in, w_back)
        back.append(exchange(out.reshape(experts, capacity, 2 * width), "expert").reshape(total, 2 * width))
        kept.append((hid, pre, g))

    order = jnp.asarray(bit_reversed(n), jnp.int32)[jnp.bitwise_xor(jnp.arange(n, dtype=jnp.int32), me)]
    assert micros == 2
    cols = ff // n
    grad_back = pl.pallas_call(
        grad_back_kernel,
        out_shape=jax.ShapeDtypeStruct((n, cols, width), bf16),
        grid_spec=pltpu.PrefetchScalarGridSpec(
            num_scalar_prefetch=1,
            grid=(n,),
            in_specs=[
                pl.BlockSpec((total, cols), lambda b, pos: (0, b)),
                pl.BlockSpec((total, cols), lambda b, pos: (0, b)),
                pl.BlockSpec((total, width), lambda b, pos: (0, 0)),
                pl.BlockSpec((total, width), lambda b, pos: (0, 0)),
            ],
            out_specs=pl.BlockSpec((None, cols, width), lambda b, pos: (pos[b], 0, 0)),
        ),
        compiler_params=pltpu.CompilerParams(vmem_limit_bytes=48 * MIB),
        cost_estimate=pl.CostEstimate(
            flops=4 * total * width * ff, transcendentals=0, bytes_accessed=12 * MIB
        ),
        name="grad_back",
    )(order, kept[0][0], kept[1][0], kept[0][2], kept[1][2])
    grad_in = pl.pallas_call(
        grad_in_kernel,
        out_shape=jax.ShapeDtypeStruct((n, width // n, ff), bf16),
        grid_spec=pltpu.PrefetchScalarGridSpec(
            num_scalar_prefetch=1,
            grid=(ff // tile,),
            in_specs=[
                pl.BlockSpec((total, width), lambda f, pos: (0, 0)),
                pl.BlockSpec((total, width), lambda f, pos: (0, 0)),
                pl.BlockSpec((total, tile), lambda f, pos: (0, f)),
                pl.BlockSpec((total, tile), lambda f, pos: (0, f)),
            ],
            out_specs=pl.BlockSpec((n, width // n, tile), lambda f, pos: (0, 0, f)),
        ),
        compiler_params=pltpu.CompilerParams(vmem_limit_bytes=48 * MIB),
        cost_estimate=pl.CostEstimate(
            flops=4 * total * width * ff, transcendentals=0, bytes_accessed=12 * MIB
        ),
        name="grad_in",
    )(order, arrived[0], arrived[1], kept[0][1], kept[1][1])
    grad_back = halving_sum(grad_back, "dp")
    grad_in = halving_sum(grad_in, "dp")

    outputs = []
    token_grads = []
    dense_grad = ()
    attn_grad = ()
    for m in range(micros):
        first, last = m == 0, m == micros - 1
        out, da, mixed_grad, *dense_grad = call(
            functools.partial(combine_kernel, m, first),
            [
                ((tok, width), bf16),
                ((n, tok, part), bf16),
                ((tok, width), f32),
                ((width, width + LANES), bf16 if last else f32),
            ],
            "combine",
            flops=6 * total * tok * width + 4 * tok * width * width,
            n_in=8 + len(dense_grad),
        )(back[m], places, routes, mixed[m], cotangent, att[m], dense, gain_f, *dense_grad)
        outputs.append(out)
        da = exchange(da, "dp")
        kdoc, qdoc, qkv, lse = saved[m]
        *parts, grad_w, grad_gain, grad_band = call(
            functools.partial(attn_bwd_kernel, m, n, reach, heads, first),
            [((tok, width), bf16)] * n
            + [
                ((width, 3 * wide), bf16 if last else f32),
                ((8, width), f32),
                ((8, spans * tok), f32),
            ],
            "attention_backward",
            flops=4 * length * width * 3 * wide + 5 * pair_flops,
            scratch=[
                pltpu.VMEM((length, width), bf16),
                pltpu.VMEM((groups, length, LANES), bf16),
                pltpu.VMEM((wide, length), bf16),
                pltpu.VMEM((wide, length), f32),
                pltpu.VMEM((2 * groups, length, LANES), f32),
                pltpu.VMEM((length, 3 * wide), bf16),
                pltpu.VMEM((heads, spans, tok, tok), f32),
            ],
            n_smem=1,
            n_in=8 + n + len(attn_grad),
        )(idx, gain_a, w_heads, tiles, kdoc, qdoc, qkv, lse, da, *xs, *attn_grad)
        attn_grad = (grad_w, grad_gain, grad_band)
        summed = [parts[0]] + [swap(parts[r], "dp", r) for r in range(1, n)]
        (token_grad,) = call(
            functools.partial(token_grad_kernel, m),
            [((tok, width), bf16)],
            "token_grad",
            n_in=3 + n,
        )(tokens, mixed_grad, gain_a, *summed)
        token_grads.append(token_grad)

    whole_count = n * experts
    dense_sum = exchange(dense_grad[0].reshape(whole_count, own_rows, width + LANES), both)
    dense_sum = jnp.sum(dense_sum.astype(f32), axis=0)
    band_flat = grad_band[:heads, :WINDOW].astype(bf16)
    band_width = band_flat.shape[1]
    per_row = -(-heads * band_width // (own_rows * LANES)) * LANES
    band_flat = jnp.pad(band_flat.reshape(-1), (0, own_rows * per_row - heads * band_width))
    band_flat = jnp.broadcast_to(
        band_flat.reshape(1, own_rows, per_row), (whole_count, own_rows, per_row)
    )
    grad_w = grad_w.reshape(width, 3, wide)[:, :, :part].reshape(width, 3 * part)
    message = jnp.concatenate(
        [
            grad_w,
            grad_gain[0].astype(bf16)[:, None],
            jnp.zeros((width, send_cols - 3 * part - 1), bf16),
        ],
        axis=1,
    ).reshape(whole_count, own_rows, send_cols)
    message = exchange(jnp.concatenate([message, band_flat], axis=2), both)
    message = message.reshape(n, experts, own_rows, send_cols + per_row).astype(f32)
    by_dp = jnp.sum(message, axis=1)
    grad_qkv = by_dp[:, :, : 3 * part].reshape(n, own_rows, 3, part).transpose(1, 2, 0, 3)
    grad_qkv = grad_qkv.reshape(own_rows, 3, n * part)[:, :, :width].reshape(own_rows, 3 * width)
    grad_gain_a = jnp.sum(by_dp[:, :, 3 * part], axis=0)
    grad_bias = by_dp[:, :, send_cols:].reshape(n, own_rows * per_row)[:, : heads * band_width]
    grad_bias = grad_bias.reshape(n * heads, band_width)[:H].T
    grad_bias = jnp.pad(grad_bias, ((0, WINDOW - band_width), (0, 0)))
    return (
        jnp.stack(outputs)[:, None],
        jnp.stack(token_grads)[:, None],
        grad_qkv,
        dense_sum[:, :width],
        grad_bias,
        grad_gain_a,
        dense_sum[:, width + LANES - 1],
        dense_sum[:, width : width + experts],
        grad_in[None],
        grad_back[None],
    )


def solution(mesh):
    return jax.shard_map(
        shards,
        mesh=mesh,
        in_specs=(
            P(None, "expert", "dp", None),
            P(None, "expert", None),
            P(None, "expert", "dp", None),
            P(None, "expert", "dp", None),
            P(("dp", "expert"), None),
            P(("dp", "expert"), None),
            P(),
            P(("dp", "expert")),
            P(("dp", "expert")),
            P(("dp", "expert"), None),
            P("expert", None, None),
            P("expert", None, None),
            P(None, "expert", "dp", None),
        ),
        out_specs=(
            P(None, "expert", "dp", None),
            P(None, "expert", "dp", None),
            P(("dp", "expert"), None),
            P(("dp", "expert"), None),
            P(),
            P(("dp", "expert")),
            P(("dp", "expert")),
            P(("dp", "expert"), None),
            P("expert", "dp", None),
            P("expert", "dp", None),
        ),
        check_vma=False,
    )
```

time: 1620 us -> 564 us (0.35); the launches traced: 1590 us -> 555 us
  local copies, waits for them, and re-layouts: 569 us -> 79.3 us
  waiting for transfers between devices: 504 us -> 202 us
  matrix products: 221 us -> 0 us
  Pallas kernels: 0 us -> 142 us
  blocking collectives: 135 us -> 28.4 us
  other arithmetic: 94.1 us -> 25.3 us
    reduce_scatter x4 -> x0, waiting for transfers between devices: 322 us -> none  [the longest x1 125 us: shards(): lax.psum_scatter(grad_qkv, ('dp', 'expert'), scatter_dimension=0, tiled=T...]
    rev x9 -> x1, local copies, waits for them, and re-layouts: 262 us -> 0.35 us  [shards(): other_row = routes[..., ::-1].transpose(0, 2, 1)]
    dot_general x72 -> x0, matrix products: 221 us -> none  [the longest x6 25.1 us: shards(): jnp.einsum('hqk,qhd->khd', prob_low, grad_part, preferred_element_type=jn...]
    pallas_call x0 -> x16, Pallas kernels: none -> 142 us  [the longest x2 38.8 us: shards(): call(functools.partial(attn_bwd_kernel, m, n, reach, heads, first), [((to...]
    reshape x11 -> x7, local copies, waits for them, and re-layouts: 100 us -> 4.12 us  [the longest x2 1.9 us: shards(): att.append(exchange(att_m.reshape(n, tok, part), 'dp'))]
    psum x1 -> x0, waiting for transfers between devices: 84.3 us -> none  [shards(): lax.psum(band_grad[:, tok_rows - 1:tok_rows - 1 + WINDOW].T, ('dp', 'expe...]
    ppermute x12 -> x13, waiting for transfers between devices: 16.7 us -> 98.1 us  [swap(): lax.ppermute(x, axis, [(i, i ^ by) for i in range(lax.axis_size(axis))])]
    all_gather x1 -> x0, blocking collectives: 66.3 us -> none  [collect_dense(): lax.all_gather(w_router, ('dp', 'expert'), axis=0, tiled=True)]
  transfers between devices with their start and end apart: 26 -> 26, of which waited for: 14 -> 12; matrix products, arithmetic and copies ran while one was open for 31% -> 11% of each run, Pallas kernels for 0% -> 24%
where the time goes in v1:
time: 564 us; the launch traced here: 555 us
  waiting for transfers between devices  202 us (36%)
  Pallas kernels  142 us (25%)
  local copies, waits for them, and re-layouts  79.3 us (14%)
  starting transfers between devices  63.5 us (11%)
  blocking collectives  28.4 us (5%)
  other arithmetic  25.3 us (4%)
  between operations  15.2 us (3%)
    all_to_all x12, waiting for transfers between devices, exchange(): return lax.all_to_all(x, axes, split_axis=0, concat_axis=0, tiled=True)  104 us
    ppermute x13, waiting for transfers between devices, swap(): lax.ppermute(x, axis, [(i, i ^ by) for i in range(lax.axis_size(axis))])  98.1 us
    all_to_all x12, starting transfers between devices, exchange(): return lax.all_to_all(x, axes, split_axis=0, concat_axis=0, tiled=True)  55.4 us
    pallas_call x2, Pallas kernels, shards(): call(functools.partial(attn_bwd_kernel, m, n, reach, heads, first), [((to...  38.8 us
    pallas_call x2, Pallas kernels, shards(): pl.pallas_call(functools.partial(expert_kernel, m), out_shape=[jax.ShapeD...  36.8 us
    unnamed x120, local copies, waits for them, and re-layouts  35.4 us
    all_to_all x1, blocking collectives, exchange(): return lax.all_to_all(x, axes, split_axis=0, concat_axis=0, tiled=True)  28.4 us
    pallas_call x2, Pallas kernels, shards(): call(functools.partial(attn_fwd_kernel, m, n, reach, heads), [((length, p...  24.9 us
  transfers between devices with their start and end apart: 26, of which 12 were waited for; matrix products, arithmetic and copies ran while one was open for 11% of the time, Pallas kernels for 24%

profile of v1, /device:TPU:0, one launch (start us, length us, event | category | flops | bytes accessed | tf_op | source)
XLA Modules:
  0.0 555.5 jit_solution(5885459962976920809)
XLA Ops:
  13.6 7.4 %all-to-all-start = ((bf16[32,24,640]{2,1,0:T(8,128)(2,1)}), bf16[32,24,640]{2,1,0:T(8,128)(2,1)}, u32[]{:S(2)}, u32[]{:S(2)}) async-start(bf16[32,24,640]{2,1,0:T(8,128)(2,1)} %bitcast.4), calls=%async_computation | async-start | bytes 1966080 | tf_op jit(solution)/shard_map/all_to_all | solution.py:380
  23.2 29.1 %collective-permute-done.1.rest_2_ = bf16[2,256,768]{2,1,0:T(8,128)(2,1)} collective-permute-done((bf16[2,256,768]{2,1,0:T(8,128)(2,1)S(1)}, bf16[2,256,768]{2,1,0:T(8,128)(2,1)}, u32[]{:S(2)}, u32[]{:S(2)}) %collective-permute-start.1) | collective-permute-done | bytes 786464 | tf_op jit(solution)/shard_map/ppermute | solution.py:376
  59.6 5.4 all-to-all-start.4
  70.4 12.6 %attention_forward.2 = (bf16[1024,192]{1,0:T(8,128)(2,1)S(1)}, bf16[6,1024,128]{2,1,0:T(8,128)(2,1)}, f32[8,1024]{1,0:T(8,128)S(1)}) custom-call(s32[1]{0:T(128)} %bitcast.2.idx_ref, f32[1,768]{1,0:T(1,128)S(1)} %reshape.195.gain_ref, bf16[768,768]{1,0:T(8,128)(2,1)S(1)} %copy.166.w_ref, f32[3,4,256,256]{3,2,1,0:T(8,128)} %copy-done.6, ...), custom_call_target="tpu_custom_call" | custom-call | flops 2214592512 | bytes 4194304 | tf_op jit(solution)/shard_map/attention_forward/pallas_call | solution.py:504
  88.8 12.3 %attention_forward.3 = (bf16[1024,192]{1,0:T(8,128)(2,1)S(1)}, bf16[6,1024,128]{2,1,0:T(8,128)(2,1)}, f32[8,1024]{1,0:T(8,128)S(1)}) custom-call(s32[1]{0:T(128)} %bitcast.2.idx_ref, f32[1,768]{1,0:T(1,128)S(1)} %reshape.195.gain_ref, bf16[768,768]{1,0:T(8,128)(2,1)S(1)} %copy.166.w_ref, f32[3,4,256,256]{3,2,1,0:T(8,128)} %copy-done.6, ...), custom_call_target="tpu_custom_call" | custom-call | flops 2214592512 | bytes 4194304 | tf_op jit(solution)/shard_map/attention_forward/pallas_call | solution.py:504
  113.7 28.4 %all_to_all.65 = bf16[8,72,768]{2,1,0:T(8,128)(2,1)} all-to-all(bf16[8,72,768]{2,1,0:T(8,128)(2,1)S(1)} %bitcast.93), channel_id=1, replica_groups=mesh['dp'=4,'expert'=8] {'expert'}, dimensions={0} | all-to-all | bytes 1769472 | tf_op jit(solution)/shard_map/all_to_all | solution.py:380
  151.0 35.8 %all-to-all-done.3 = bf16[8,72,1536]{2,1,0:T(8,128)(2,1)} async-done(((bf16[8,72,1536]{2,1,0:T(8,128)(2,1)}), bf16[8,72,1536]{2,1,0:T(8,128)(2,1)}, u32[]{:S(2)}, u32[]{:S(2)}) %all-to-all-start.3) | async-done | bytes 1769504 | tf_op jit(solution)/shard_map/all_to_all | solution.py:380
  194.0 18.3 %expert.2 = (bf16[576,1536]{1,0:T(8,128)(2,1)S(1)}, bf16[576,3072]{1,0:T(8,128)(2,1)}, bf16[576,3072]{1,0:T(8,128)(2,1)}, bf16[576,768]{1,0:T(8,128)(2,1)S(1)}) custom-call(s32[1]{0:T(128)} %bitcast.e_ref, bf16[576,768]{1,0:T(8,128)(2,1)S(1)} %bitcast.90, bf16[576,1536]{1,0:T(8,128)(2,1)} %bitcast.21.c_ref, s32[576,2]{1,0:T(8,128)S(1)} %bitcast.98, ...), custom_call_target="tpu_custom_call" | custom-call | flops 10871635968 | bytes 20971520 | tf_op jit(solution)/shard_map/expert/pallas_call | solution.py:534
  214.4 6.1 %all-to-all-start.5 = ((bf16[8,72,1536]{2,1,0:T(8,128)(2,1)}), bf16[8,72,1536]{2,1,0:T(8,128)(2,1)}, u32[]{:S(2)}, u32[]{:S(2)}) async-start(bf16[8,72,1536]{2,1,0:T(8,128)(2,1)} %bitcast.87), calls=%async_computation.5 | async-start | bytes 3538944 | tf_op jit(solution)/shard_map/all_to_all | solution.py:380
  221.5 18.5 %expert.3 = (bf16[576,1536]{1,0:T(8,128)(2,1)S(1)}, bf16[576,3072]{1,0:T(8,128)(2,1)}, bf16[576,3072]{1,0:T(8,128)(2,1)}, bf16[576,768]{1,0:T(8,128)(2,1)S(1)}) custom-call(s32[1]{0:T(128)} %bitcast.e_ref, bf16[576,768]{1,0:T(8,128)(2,1)} %bitcast.32.x_ref.x1_ref, bf16[576,1536]{1,0:T(8,128)(2,1)} %bitcast.21.c_ref, s32[576,2]{1,0:T(8,128)S(1)} %bitcast.99, ...), custom_call_target="tpu_custom_call" | custom-call | flops 10871635968 | bytes 20971520 | tf_op jit(solution)/shard_map/expert/pallas_call | solution.py:534
  242.2 18.6 %all-to-all-done.5 = bf16[8,72,1536]{2,1,0:T(8,128)(2,1)} async-done(((bf16[8,72,1536]{2,1,0:T(8,128)(2,1)}), bf16[8,72,1536]{2,1,0:T(8,128)(2,1)}, u32[]{:S(2)}, u32[]{:S(2)}) %all-to-all-start.5) | async-done | bytes 1769504 | tf_op jit(solution)/shard_map/all_to_all | solution.py:380
  269.1 6.1 %combine.2 = (bf16[256,768]{1,0:T(8,128)(2,1)S(1)}, bf16[4,256,192]{2,1,0:T(8,128)(2,1)S(1)}, f32[256,768]{1,0:T(8,128)S(1)}, f32[768,896]{1,0:T(8,128)}) custom-call(bf16[576,1536]{1,0:T(8,128)(2,1)} %bitcast.27.back_ref, s32[2,256,2]{2,1,0:T(8,128)S(1)} %copy-done.4, s32[2,256,2]{2,1,0:T(8,128)S(1)} %bitcast.79, f32[256,768]{1,0:T(8,128)S(1)} %copy-done.24, ...), custom_call_target="tpu_custom_call" | custom-call | flops 1283457024 | bytes 4194304 | tf_op jit(solution)/shard_map/combine/pallas_call | solution.py:620
  277.6 28.3 %all-to-all-done.8 = bf16[8,72,1536]{2,1,0:T(8,128)(2,1)} async-done(((bf16[8,72,1536]{2,1,0:T(8,128)(2,1)}), bf16[8,72,1536]{2,1,0:T(8,128)(2,1)}, u32[]{:S(2)}, u32[]{:S(2)}) %all-to-all-start.8) | async-done | bytes 1769504 | tf_op jit(solution)/shard_map/all_to_all | solution.py:380
  309.1 7.0 %combine.3 = (bf16[256,768]{1,0:T(8,128)(2,1)S(1)}, bf16[4,256,192]{2,1,0:T(8,128)(2,1)S(1)}, f32[256,768]{1,0:T(8,128)S(1)}, bf16[768,896]{1,0:T(8,128)(2,1)}) custom-call(bf16[576,1536]{1,0:T(8,128)(2,1)} %bitcast.34.back_ref, s32[2,256,2]{2,1,0:T(8,128)S(1)} %copy-done.5, s32[2,256,2]{2,1,0:T(8,128)S(1)} %bitcast.80, f32[256,768]{1,0:T(8,128)S(1)} %copy-done.22, ...), custom_call_target="tpu_custom_call" | custom-call | flops 1283457024 | bytes 4194304 | tf_op jit(solution)/shard_map/combine/pallas_call | solution.py:620
  324.0 11.7 %grad_in.1 = bf16[4,192,3072]{2,1,0:T(8,128)(2,1)} custom-call(s32[4]{0:T(128)S(1)} %gather_fusion, bf16[576,768]{1,0:T(8,128)(2,1)S(1)} %bitcast.91, bf16[576,768]{1,0:T(8,128)(2,1)} %bitcast.32.x_ref.x1_ref, bf16[576,3072]{1,0:T(8,128)(2,1)S(1)} %copy-done.43, bf16[576,3072]{1,0:T(8,128)(2,1)} %get-tuple-element.93.p1_ref), custom_call_target="tpu_custom_call" | custom-call | flops 5435817984 | bytes 12582912 | tf_op jit(solution)/shard_map/grad_in/pallas_call | solution.py:591
  347.4 11.1 %grad_back.1 = bf16[4,768,768]{2,1,0:T(8,128)(2,1)} custom-call(s32[4]{0:T(128)S(1)} %gather_fusion, bf16[576,3072]{1,0:T(8,128)(2,1)S(1)} %copy-done.42, bf16[576,3072]{1,0:T(8,128)(2,1)} %get-tuple-element.95.h1_ref, bf16[576,768]{1,0:T(8,128)(2,1)S(1)} %copy-done.45, bf16[576,768]{1,0:T(8,128)(2,1)S(1)} %copy-done.47), custom_call_target="tpu_custom_call" | custom-call | flops 5435817984 | bytes 12582912 | tf_op jit(solution)/shard_map/grad_back/pallas_call | solution.py:571
  363.7 18.9 %attention_backward.2 = (bf16[256,768]{1,0:T(8,128)(2,1)S(1)}, bf16[256,768]{1,0:T(8,128)(2,1)S(1)}, bf16[256,768]{1,0:T(8,128)(2,1)S(1)}, bf16[256,768]{1,0:T(8...) custom-call(s32[1]{0:T(128)} %bitcast.2.idx_ref, ...), custom_call_target="tpu_custom_call" | custom-call | flops 4932501504 | bytes 4194304 | tf_op jit(solution)/shard_map/attention_backward/pallas_call | solution.py:635
  384.1 19.9 %attention_backward.3 = (bf16[256,768]{1,0:T(8,128)(2,1)S(1)}, bf16[256,768]{1,0:T(8,128)(2,1)}, bf16[256,768]{1,0:T(8,128)(2,1)S(1)}, bf16[256,768]{1,0:T(8,128...) custom-call(s32[1]{0:T(128)} %bitcast.2.idx_ref, ...), custom_call_target="tpu_custom_call" | custom-call | flops 4932501504 | bytes 4194304 | tf_op jit(solution)/shard_map/attention_backward/pallas_call | solution.py:635
  435.3 19.7 %all-to-all-done.11 = bf16[32,24,768]{2,1,0:T(8,128)(2,1)} async-done(((bf16[32,24,768]{2,1,0:T(8,128)(2,1)}), bf16[32,24,768]{2,1,0:T(8,128)(2,1)}, u32[]{:S(2)}, u32[]{:S(2)}) %all-to-all-start.11) | async-done | bytes 1179680 | tf_op jit(solution)/shard_map/all_to_all | solution.py:380
  461.7 12.1 %collective-permute-done.10 = bf16[1,192,3072]{2,1,0:T(8,128)(2,1)} collective-permute-done((bf16[1,192,3072]{2,1,0:T(8,128)(2,1)}, bf16[1,192,3072]{2,1,0:T(8,128)(2,1)}, u32[]{:S(2)}, u32[]{:S(2)}) %collective-permute-start.10) | collective-permute-done | bytes 1179680 | tf_op jit(solution)/shard_map/ppermute | solution.py:376
  473.8 30.1 %collective-permute-done.12 = bf16[1,768,768]{2,1,0:T(8,128)(2,1)} collective-permute-done((bf16[1,768,768]{2,1,0:T(8,128)(2,1)}, bf16[1,768,768]{2,1,0:T(8,128)(2,1)}, u32[]{:S(2)}, u32[]{:S(2)}) %collective-permute-start.12) | collective-permute-done | bytes 1179680 | tf_op jit(solution)/shard_map/ppermute | solution.py:376
  514.0 8.2 %collective-permute-done.8.rest_3_ = bf16[256,768]{1,0:T(8,128)(2,1)S(1)} collective-permute-done((bf16[256,768]{1,0:T(8,128)(2,1)}, bf16[256,768]{1,0:T(8,128)(2,1)S(1)}, u32[]{:S(2)}, u32[]{:S(2)}) %collective-permute-start.8) | collective-permute-done | bytes 393248 | tf_op jit(solution)/shard_map/ppermute | solution.py:376
  522.6 8.2 %collective-permute-done.4.rest_2_ = bf16[256,768]{1,0:T(8,128)(2,1)S(1)} collective-permute-done((bf16[256,768]{1,0:T(8,128)(2,1)}, bf16[256,768]{1,0:T(8,128)(2,1)S(1)}, u32[]{:S(2)}, u32[]{:S(2)}) %collective-permute-start.4) | collective-permute-done | bytes 393248 | tf_op jit(solution)/shard_map/ppermute | solution.py:376
  530.8 8.2 %collective-permute-done.5.rest_3_ = bf16[256,768]{1,0:T(8,128)(2,1)S(1)} collective-permute-done((bf16[256,768]{1,0:T(8,128)(2,1)}, bf16[256,768]{1,0:T(8,128)(2,1)S(1)}, u32[]{:S(2)}, u32[]{:S(2)}) %collective-permute-start.5) | collective-permute-done | bytes 393248 | tf_op jit(solution)/shard_map/ppermute | solution.py:376
  (243 shorter events, 158.4 us)
Async XLA Ops:
  7.2 99.6 %all-gather.2.cloned.1.call-start = ((), (), s32[]{:S(2)}) async-start(), calls=%async_computation.13 | async-start | bytes 1419264 | tf_op jit(solution)/shard_map/all_gather | solution.py:449
  13.6 46.0 %all-to-all-start = ((bf16[32,24,640]{2,1,0:T(8,128)(2,1)}), bf16[32,24,640]{2,1,0:T(8,128)(2,1)}, u32[]{:S(2)}, u32[]{:S(2)}) async-start(bf16[32,24,640]{2,1,0:T(8,128)(2,1)} %bitcast.4), calls=%async_computation | async-start | bytes 1966080 | tf_op jit(solution)/shard_map/all_to_all | solution.py:380
  21.1 31.3 %collective-permute-start.1 = (bf16[2,256,768]{2,1,0:T(8,128)(2,1)S(1)}, bf16[2,256,768]{2,1,0:T(8,128)(2,1)}, u32[]{:S(2)}, u32[]{:S(2)}) collective-permute-start(bf16[2,256,768]{2,1,0:T(8,128)(2,1)S(1)} %bitcast.68), channel_id=1, source_target_pairs={{0,16},{8,24},{16,0},{24,8},{1,17},{9,25},{17,1},{25,9},{2,18},{10... | collective-permute-start | bytes 2359304 | tf_op jit(solution)/shard_map/ppermute | solution.py:376
  22.8 47.6 %collective-permute-start = (bf16[2,256,768]{2,1,0:T(8,128)(2,1)S(1)}, bf16[2,256,768]{2,1,0:T(8,128)(2,1)}, u32[]{:S(2)}, u32[]{:S(2)}) collective-permute-start(bf16[2,256,768]{2,1,0:T(8,128)(2,1)S(1)} %bitcast.69), channel_id=1, source_target_pairs={{0,8},{8,0},{16,24},{24,16},{1,9},{9,1},{17,25},{25,17},{2,10},{10... | collective-permute-start | bytes 2359304 | tf_op jit(solution)/shard_map/ppermute | solution.py:376
  59.6 24.3 %all-to-all-start.4 = ((s32[8,2,72]{2,1,0:T(2,128)}), s32[8,2,72]{2,1,0:T(2,128)S(1)}, u32[]{:S(2)}, u32[]{:S(2)}) async-start(s32[8,2,72]{2,1,0:T(2,128)} %bitcast.23), calls=%async_computation.4 | async-start | bytes 16384 | tf_op jit(solution)/shard_map/all_to_all | solution.py:380
  84.0 18.1 %all-to-all-start.1 = ((bf16[4,256,192]{1,2,0:T(8,128)(2,1)}), bf16[4,256,192]{1,2,0:T(8,128)(2,1)}, u32[]{:S(2)}, u32[]{:S(2)}) async-start(bf16[4,256,192]{1,2,0:T(8,128)(2,1)} %copy.168), calls=%async_computation.1 | async-start | bytes 786432 | tf_op jit(solution)/shard_map/all_to_all | solution.py:380
  142.2 44.6 %all-to-all-start.3 = ((bf16[8,72,1536]{2,1,0:T(8,128)(2,1)}), bf16[8,72,1536]{2,1,0:T(8,128)(2,1)}, u32[]{:S(2)}, u32[]{:S(2)}) async-start(bf16[8,72,1536]{2,1,0:T(8,128)(2,1)} %bitcast.85), calls=%async_computation.3 | async-start | bytes 3538944 | tf_op jit(solution)/shard_map/all_to_all | solution.py:380
  186.7 27.7 %all-to-all-start.7 = ((bf16[8,72,768]{2,1,0:T(8,128)(2,1)}), bf16[8,72,768]{2,1,0:T(8,128)(2,1)}, u32[]{:S(2)}, u32[]{:S(2)}) async-start(bf16[8,72,768]{2,1,0:T(8,128)(2,1)} %bitcast.92), calls=%async_computation.7 | async-start | bytes 1769472 | tf_op jit(solution)/shard_map/all_to_all | solution.py:380
  214.4 46.4 %all-to-all-start.5 = ((bf16[8,72,1536]{2,1,0:T(8,128)(2,1)}), bf16[8,72,1536]{2,1,0:T(8,128)(2,1)}, u32[]{:S(2)}, u32[]{:S(2)}) async-start(bf16[8,72,1536]{2,1,0:T(8,128)(2,1)} %bitcast.87), calls=%async_computation.5 | async-start | bytes 3538944 | tf_op jit(solution)/shard_map/all_to_all | solution.py:380
  260.8 45.1 %all-to-all-start.8 = ((bf16[8,72,1536]{2,1,0:T(8,128)(2,1)}), bf16[8,72,1536]{2,1,0:T(8,128)(2,1)}, u32[]{:S(2)}, u32[]{:S(2)}) async-start(bf16[8,72,1536]{2,1,0:T(8,128)(2,1)} %bitcast.86), calls=%async_computation.8 | async-start | bytes 3538944 | tf_op jit(solution)/shard_map/all_to_all | solution.py:380
  317.9 22.6 %all-to-all-start.10 = ((bf16[4,256,192]{1,2,0:T(8,128)(2,1)}), bf16[4,256,192]{1,2,0:T(8,128)(2,1)}, u32[]{:S(2)}, u32[]{:S(2)}) async-start(bf16[4,256,192]{1,2,0:T(8,128)(2,1)} %copy.186), calls=%async_computation.10 | async-start | bytes 786432 | tf_op jit(solution)/shard_map/all_to_all | solution.py:380
  339.1 85.5 %collective-permute-start.9 = (bf16[2,192,3072]{2,1,0:T(8,128)(2,1)}, bf16[2,192,3072]{2,1,0:T(8,128)(2,1)}, u32[]{:S(2)}, u32[]{:S(2)}) collective-permute-start(bf16[2,192,3072]{2,1,0:T(8,128)(2,1)} %slice.109), channel_id=1, source_target_pairs={{0,8},{8,0},{16,24},{24,16},{1,9},{9,1},{17,25},{25,17},{2,10},{10... | collective-permute-start | bytes 7077896 | tf_op jit(solution)/shard_map/ppermute | solution.py:376
  340.5 23.0 %all-to-all-start.9 = ((bf16[4,256,192]{1,2,0:T(8,128)(2,1)}), bf16[4,256,192]{1,2,0:T(8,128)(2,1)S(1)}, u32[]{:S(2)}, u32[]{:S(2)}) async-start(bf16[4,256,192]{1,2,0:T(8,128)(2,1)} %copy.182), calls=%async_computation.9 | async-start | bytes 786432 | tf_op jit(solution)/shard_map/all_to_all | solution.py:380
  361.8 69.2 %collective-permute-start.11 = (bf16[2,768,768]{2,1,0:T(8,128)(2,1)}, bf16[2,768,768]{2,1,0:T(8,128)(2,1)}, u32[]{:S(2)}, u32[]{:S(2)}) collective-permute-start(bf16[2,768,768]{2,1,0:T(8,128)(2,1)} %slice.113), channel_id=1, source_target_pairs={{0,8},{8,0},{16,24},{24,16},{1,9},{9,1},{17,25},{25,17},{2,10},{10... | collective-permute-start | bytes 7077896 | tf_op jit(solution)/shard_map/ppermute | solution.py:376
  420.6 34.4 %all-to-all-start.11 = ((bf16[32,24,768]{2,1,0:T(8,128)(2,1)}), bf16[32,24,768]{2,1,0:T(8,128)(2,1)}, u32[]{:S(2)}, u32[]{:S(2)}) async-start(bf16[32,24,768]{2,1,0:T(8,128)(2,1)} %pad_maximum_fusion), calls=%async_computation.11 | async-start | bytes 2359296 | tf_op jit(solution)/shard_map/all_to_all | solution.py:380
  429.3 44.5 %collective-permute-start.10 = (bf16[1,192,3072]{2,1,0:T(8,128)(2,1)}, bf16[1,192,3072]{2,1,0:T(8,128)(2,1)}, u32[]{:S(2)}, u32[]{:S(2)}) collective-permute-start(bf16[1,192,3072]{2,1,0:T(8,128)(2,1)} %slice.111), channel_id=1, source_target_pairs={{0,16},{8,24},{16,0},{24,8},{1,17},{9,25},{17,1},{25,9},{2,18},{10... | collective-permute-start | bytes 3538952 | tf_op jit(solution)/shard_map/ppermute | solution.py:376
  435.0 68.8 %collective-permute-start.12 = (bf16[1,768,768]{2,1,0:T(8,128)(2,1)}, bf16[1,768,768]{2,1,0:T(8,128)(2,1)}, u32[]{:S(2)}, u32[]{:S(2)}) collective-permute-start(bf16[1,768,768]{2,1,0:T(8,128)(2,1)} %slice.115), channel_id=1, source_target_pairs={{0,16},{8,24},{16,0},{24,8},{1,17},{9,25},{17,1},{25,9},{2,18},{10... | collective-permute-start | bytes 3538952 | tf_op jit(solution)/shard_map/ppermute | solution.py:376
  455.0 89.6 %all-to-all-start.12 = ((bf16[32,24,896]{2,1,0:T(8,128)(2,1)}), bf16[32,24,896]{2,1,0:T(8,128)(2,1)}, u32[]{:S(2)}, u32[]{:S(2)}) async-start(bf16[32,24,896]{2,1,0:T(8,128)(2,1)} %bitcast.45), calls=%async_computation.12 | async-start | bytes 2752512 | tf_op jit(solution)/shard_map/all_to_all | solution.py:380
  458.7 46.4 %collective-permute-start.6 = (bf16[256,768]{1,0:T(8,128)(2,1)}, bf16[256,768]{1,0:T(8,128)(2,1)S(1)}, u32[]{:S(2)}, u32[]{:S(2)}) collective-permute-start(bf16[256,768]{1,0:T(8,128)(2,1)} %get-tuple-element.85), channel_id=1, source_target_pairs={{0,8},{8,0},{16,24},{24,16},{1,9},{9,1},{17,25},{25,17},{2,10},{10... | collective-permute-start | bytes 1179656 | tf_op jit(solution)/shard_map/ppermute | solution.py:376
  460.0 54.0 %collective-permute-start.7 = (bf16[256,768]{1,0:T(8,128)(2,1)}, bf16[256,768]{1,0:T(8,128)(2,1)S(1)}, u32[]{:S(2)}, u32[]{:S(2)}) collective-permute-start(bf16[256,768]{1,0:T(8,128)(2,1)} %copy-done.39), channel_id=1, source_target_pairs={{0,16},{8,24},{16,0},{24,8},{1,17},{9,25},{17,1},{25,9},{2,18},{10... | collective-permute-start | bytes 1179656 | tf_op jit(solution)/shard_map/ppermute | solution.py:376
  461.7 60.5 %collective-permute-start.8 = (bf16[256,768]{1,0:T(8,128)(2,1)}, bf16[256,768]{1,0:T(8,128)(2,1)S(1)}, u32[]{:S(2)}, u32[]{:S(2)}) collective-permute-start(bf16[256,768]{1,0:T(8,128)(2,1)} %copy-done.38), channel_id=1, source_target_pairs={{0,24},{8,16},{16,8},{24,0},{1,25},{9,17},{17,9},{25,1},{2,26},{10... | collective-permute-start | bytes 1179656 | tf_op jit(solution)/shard_map/ppermute | solution.py:376
  473.7 48.9 %collective-permute-start.3 = (bf16[256,768]{1,0:T(8,128)(2,1)}, bf16[256,768]{1,0:T(8,128)(2,1)S(1)}, u32[]{:S(2)}, u32[]{:S(2)}) collective-permute-start(bf16[256,768]{1,0:T(8,128)(2,1)} %copy-done.37), channel_id=1, source_target_pairs={{0,8},{8,0},{16,24},{24,16},{1,9},{9,1},{17,25},{25,17},{2,10},{10... | collective-permute-start | bytes 1179656 | tf_op jit(solution)/shard_map/ppermute | solution.py:376
  503.8 27.0 %collective-permute-start.4 = (bf16[256,768]{1,0:T(8,128)(2,1)}, bf16[256,768]{1,0:T(8,128)(2,1)S(1)}, u32[]{:S(2)}, u32[]{:S(2)}) collective-permute-start(bf16[256,768]{1,0:T(8,128)(2,1)} %copy-done.36), channel_id=1, source_target_pairs={{0,16},{8,24},{16,0},{24,8},{1,17},{9,25},{17,1},{25,9},{2,18},{10... | collective-permute-start | bytes 1179656 | tf_op jit(solution)/shard_map/ppermute | solution.py:376
  505.1 33.9 %collective-permute-start.5 = (bf16[256,768]{1,0:T(8,128)(2,1)}, bf16[256,768]{1,0:T(8,128)(2,1)S(1)}, u32[]{:S(2)}, u32[]{:S(2)}) collective-permute-start(bf16[256,768]{1,0:T(8,128)(2,1)} %copy-done.35), channel_id=1, source_target_pairs={{0,24},{8,16},{16,8},{24,0},{1,25},{9,17},{17,9},{25,1},{2,26},{10... | collective-permute-start | bytes 1179656 | tf_op jit(solution)/shard_map/ppermute | solution.py:376
  (60 other events, 464.0 us)
Sparse Core Ops, SparseCore 0:
  11.6 59.2 all-gather.1
